TPU v7x, 256 devices: a whole 4x4x8 slice. The times are simulated.
256 devices in a mesh: clique: 4 (over x), group: 64 (over z, y, core).
Axes of the slice: x: 4, y: 4, z: 8, core: 2. Of those that a mesh axis runs over, the one named last changes fastest.
Arguments:
- hot_shard: bfloat16 [65536, 128], P('clique'), may hold values from -6 to 6
- cold_shard: bfloat16 [1048576, 128], P('group'), may hold values from -6 to 6
- hot_ids: int32 [256, 4, 512], P(('clique', 'group')), may hold values from 0 to 16383
- cold_ids: int32 [256, 64, 32], P(('clique', 'group')), may hold values from 0 to 16383
- cold_counts: int32 [256, 64], P(('clique', 'group')), may hold values from 16 to 32, as said below
- mid_self: int32 [256, 7680], P(('clique', 'group')), may hold values from 0 to 4095, as said below
- nbr1: int32 [256, 10, 7680], P(('clique', 'group')), may hold values from 0 to 4095, as said below
- nbr2: int32 [256, 15, 512], P(('clique', 'group')), may hold values from 0 to 7679
- labels: int32 [256, 512], P(('clique', 'group')), may hold values from 0 to 171
- w1_self: bfloat16 [128, 256], replicated, may hold values from -0.5 to 0.5
- w1_neigh: bfloat16 [128, 256], replicated, may hold values from -0.5 to 0.5
- w2_self: bfloat16 [256, 172], replicated, may hold values from -1.5 to 1.5
- w2_neigh: bfloat16 [256, 172], replicated, may hold values from -1.5 to 1.5
Outputs:
- seed_loss: float32 [256, 512], P(('clique', 'group'))
- grad_w1_self: float32 [128, 256], replicated
- grad_w1_neigh: float32 [128, 256], replicated
- grad_w2_self: float32 [256, 172], replicated
- grad_w2_neigh: float32 [256, 172], replicated
Inputs may be any that keep to these rules, and one draw needn't show every extreme that they name: `cold_counts`: the last store device has 32 live slots from every trainer; the other counts vary from store device to store device. `mid_self`: each entry is a position in the trainer's inputs that holds a hot row or a live cold slot. `nbr1`: each entry is a position in the trainer's inputs that holds a hot row or a live cold slot.
All inputs are finite; a program needn't handle non-finite values.
Results may differ from a plain program's by a relative error of at most 0.0021.
Values may be sent and summed in bfloat16 or wider, within the bound.
No kernel may reach another device: no remote copies, remote signals or barrier semaphores. Data moves between devices by JAX's collectives and lax.ppermute only.
A program may use at most 128 MiB of HBM per device.

v0:
```python
from functools import partial

import jax
import jax.numpy as jnp
from jax import lax
from jax.sharding import PartitionSpec as P


def neighbour_total(positions, table):
    fan_count, middle = positions.shape
    table_rows = table.shape[0]
    row_block = 512
    columns = jnp.arange(table_rows, dtype=jnp.int32)[None, None, :]
    stacked = positions.reshape(fan_count, middle // row_block, row_block).transpose(1, 0, 2)

    def one_block(block_positions):
        matches = jnp.sum((block_positions[:, :, None] == columns).astype(jnp.float32), axis=0)
        return jnp.dot(matches.astype(jnp.bfloat16), table, preferred_element_type=jnp.float32)

    totals = lax.map(one_block, stacked)
    return totals.reshape(middle, table.shape[1])


def sage_step(
    self_first, neigh_first, seed_neigh, seed_labels, w1_self, w1_neigh, w2_self, w2_neigh
):
    seeds = seed_labels.shape[0]
    fan_second = seed_neigh.shape[0]
    middle = self_first.shape[0]
    classes = w2_self.shape[1]
    pre_first = jnp.dot(self_first, w1_self, preferred_element_type=jnp.float32) + jnp.dot(
        neigh_first, w1_neigh, preferred_element_type=jnp.float32
    )
    hidden_first = jax.nn.gelu(pre_first, approximate=True).astype(jnp.bfloat16)
    node_index = jnp.arange(middle, dtype=jnp.int32)[None, None, :]
    seed_counts = jnp.sum((seed_neigh[:, :, None] == node_index).astype(jnp.float32), axis=0)
    neigh_second = (
        jnp.dot(seed_counts.astype(jnp.bfloat16), hidden_first, preferred_element_type=jnp.float32)
        / fan_second
    ).astype(jnp.bfloat16)
    seed_hidden = hidden_first[:seeds]
    logits = jnp.dot(seed_hidden, w2_self, preferred_element_type=jnp.float32) + jnp.dot(
        neigh_second, w2_neigh, preferred_element_type=jnp.float32
    )
    log_total = jnp.log(jnp.sum(jnp.exp(logits), axis=1))
    picked = jnp.take_along_axis(logits, seed_labels[:, None], axis=1)[:, 0]
    seed_loss = log_total - picked
    onehot = (seed_labels[:, None] == jnp.arange(classes, dtype=jnp.int32)[None, :]).astype(
        jnp.float32
    )
    probs = jnp.exp(logits - log_total[:, None])
    grad_logits = ((probs - onehot) / seeds).astype(jnp.bfloat16)
    term_w2_self = jnp.dot(seed_hidden.T, grad_logits, preferred_element_type=jnp.float32)
    term_w2_neigh = jnp.dot(neigh_second.T, grad_logits, preferred_element_type=jnp.float32)
    back_second = jnp.dot(grad_logits, w2_neigh.T, preferred_element_type=jnp.float32) / fan_second
    grad_hidden = lax.dot_general(
        seed_counts,
        back_second,
        (((0,), (0,)), ((), ())),
        precision=lax.Precision.HIGHEST,
        preferred_element_type=jnp.float32,
    )
    grad_hidden = grad_hidden.at[:seeds].add(
        jnp.dot(grad_logits, w2_self.T, preferred_element_type=jnp.float32)
    )
    unused, pullback = jax.vjp(partial(jax.nn.gelu, approximate=True), pre_first)
    grad_pre = pullback(grad_hidden)[0].astype(jnp.bfloat16)
    term_w1_self = jnp.dot(self_first.T, grad_pre, preferred_element_type=jnp.float32)
    term_w1_neigh = jnp.dot(neigh_first.T, grad_pre, preferred_element_type=jnp.float32)
    return (seed_loss, term_w1_self, term_w1_neigh, term_w2_self, term_w2_neigh)


def body(
    hot_shard,
    cold_shard,
    hot_ids,
    cold_ids,
    cold_counts,
    mid_self,
    nbr1,
    nbr2,
    labels,
    w1_self,
    w1_neigh,
    w2_self,
    w2_neigh,
):
    feature_width = hot_shard.shape[1]
    requests = lax.all_to_all(hot_ids[0], "clique", split_axis=0, concat_axis=0, tiled=True)
    served = jnp.take(hot_shard, requests, axis=0)
    hot_rows = lax.all_to_all(served, "clique", split_axis=0, concat_axis=0, tiled=True).reshape(
        -1, feature_width
    )
    fetched = lax.all_to_all(
        jnp.take(
            cold_shard,
            lax.all_to_all(cold_ids[0], "group", split_axis=0, concat_axis=0, tiled=True),
            axis=0,
        ),
        "group",
        split_axis=0,
        concat_axis=0,
        tiled=True,
    )
    cold_slots = fetched.shape[1]
    live_mask = jnp.arange(cold_slots, dtype=jnp.int32)[None, :] < cold_counts[0][:, None]
    cold_rows = jnp.where(live_mask[:, :, None], fetched, jnp.zeros_like(fetched)).reshape(
        -1, feature_width
    )
    fan_first = nbr1.shape[1]
    inputs = jnp.concatenate([hot_rows, cold_rows], axis=0)
    self_first = jnp.take(inputs, mid_self[0], axis=0)
    summed = neighbour_total(nbr1[0], inputs)
    neigh_first = (summed / fan_first).astype(jnp.bfloat16)
    seed_loss, term_a, term_b, term_c, term_d = sage_step(
        self_first, neigh_first, nbr2[0], labels[0], w1_self, w1_neigh, w2_self, w2_neigh
    )
    totals = lax.psum((term_a, term_b, term_c, term_d), ("clique", "group"))
    return (seed_loss[None], totals[0], totals[1], totals[2], totals[3])


def solution(mesh):
    return jax.shard_map(
        body,
        mesh=mesh,
        in_specs=(
            P("clique", None),
            P("group", None),
            P(("clique", "group"), None, None),
            P(("clique", "group"), None, None),
            P(("clique", "group"), None),
            P(("clique", "group"), None),
            P(("clique", "group"), None, None),
            P(("clique", "group"), None, None),
            P(("clique", "group"), None),
            P(),
            P(),
            P(),
            P(),
        ),
        out_specs=(P(("clique", "group"), None), P(), P(), P(), P()),
        check_vma=False,
    )
```

profile of v0, /device:TPU:1, one launch (start us, length us, event | category | flops | bytes accessed | tf_op | source)
XLA Modules:
  0.0 952.2 jit_solution(10398304202761457901)
XLA Ops:
  8.6 13.2 %all-to-all-start.2 = ((s32[64,1,32]{2,1,0:T(1,128)}), s32[64,1,32]{2,1,0:T(1,128)S(1)}, u32[]{:S(2)}, u32[]{:S(2)}) async-start(s32[64,1,32]{2,1,0:T(1,128)} %bitcast.5), calls=%async_computation.2 | async-start | bytes 65536 | tf_op jit(solution)/shard_map/all_to_all | solution.py:97
  24.2 83.1 %convert_reduce_fusion.1 = f32[512,7680]{1,0:T(8,128)} fusion(s32[15,512]{1,0:T(8,128)S(1)} %bitcast.81), kind=kLoop, calls=%fused_computation.13 | loop fusion | flops 173015040 | bytes 15759360 | tf_op jit(solution)/shard_map/reduce_sum | solution.py:36
  112.0 8.3 gather_fusion.1
  121.5 10.6 %all-to-all-start.3 = ((bf16[64,32,128]{2,1,0:T(8,128)(2,1)}), bf16[64,32,128]{2,1,0:T(8,128)(2,1)S(1)}, u32[]{:S(2)}, u32[]{:S(2)}) async-start(bf16[64,32,128]{2,1,0:T(8,128)(2,1)} %broadcast_select_fusion.3), calls=%async_computation.3 | async-start | bytes 1048576 | tf_op jit(solution)/shard_map/all_to_all | solution.py:94
  132.2 8.3 gather_fusion
  141.7 8.1 all-to-all-done.3
  149.8 4.5 all-to-all-start.1
  155.8 7.4 all-to-all-done.1
  163.3 14.4 %gather_fusion.2 = bf16[7680,128]{1,0:T(8,128)(2,1)S(1)} fusion(bf16[4096,128]{1,0:T(8,128)(2,1)S(1)} %pad_maximum_fusion, s32[8192]{0:T(1024)S(1)} %pad_clamp_fusion), kind=kCustom, calls=%fused_computation.2 | custom fusion | bytes 3962880 | tf_op jit(solution)/shard_map/jit(_take)/gather | solution.py:112
  177.7 451.1 %while.12 = (s32[]{:T(128)}, f32[15,512,128]{2,1,0:T(8,128)}, s32[15,10,512]{2,0,1:T(8,128)S(1)}, bf16[4096,128]{1,0:T(8,128)(2,1)S(1)}, s32[]{:T(128)}) while((s32[]{:T(128)}, f32[15,512,128]{2,1,0:T(8,128)}, s32[15,10,512]{2,0,1:T(8,128)S(1)}, bf16[4096,128]{1,0:T(8,128)(2,1)S(1)}, s32[]{:T(128)}) %tuple.41), condition=%wide.region_2.3_spmd.clone, body=%wide.region_0.0_spmd.clone.sunk | while | flops 597688320 | bytes 9801805 | solution.py:20
  177.7 25.9 %convert_reduce_fusion.3 = bf16[512,4096]{1,0:T(8,128)(2,1)} fusion(s32[10,512]{1,0:T(8,128)S(1)} %bitcast.73), kind=kLoop, calls=%fused_computation.6.clone.1 | loop fusion | flops 60817408 | bytes 4214784 | tf_op jit(solution)/shard_map/while/body/eval_jaxpr/reduce_sum | solution.py:17
  207.8 25.9 %convert_reduce_fusion.3 = bf16[512,4096]{1,0:T(8,128)(2,1)} fusion(s32[10,512]{1,0:T(8,128)S(1)} %bitcast.73), kind=kLoop, calls=%fused_computation.6.clone.1 | loop fusion | flops 60817408 | bytes 4214784 | tf_op jit(solution)/shard_map/while/body/eval_jaxpr/reduce_sum | solution.py:17
  237.9 25.9 %convert_reduce_fusion.3 = bf16[512,4096]{1,0:T(8,128)(2,1)} fusion(s32[10,512]{1,0:T(8,128)S(1)} %bitcast.73), kind=kLoop, calls=%fused_computation.6.clone.1 | loop fusion | flops 60817408 | bytes 4214784 | tf_op jit(solution)/shard_map/while/body/eval_jaxpr/reduce_sum | solution.py:17
  268.0 25.9 %convert_reduce_fusion.3 = bf16[512,4096]{1,0:T(8,128)(2,1)} fusion(s32[10,512]{1,0:T(8,128)S(1)} %bitcast.73), kind=kLoop, calls=%fused_computation.6.clone.1 | loop fusion | flops 60817408 | bytes 4214784 | tf_op jit(solution)/shard_map/while/body/eval_jaxpr/reduce_sum | solution.py:17
  298.1 25.9 %convert_reduce_fusion.3 = bf16[512,4096]{1,0:T(8,128)(2,1)} fusion(s32[10,512]{1,0:T(8,128)S(1)} %bitcast.73), kind=kLoop, calls=%fused_computation.6.clone.1 | loop fusion | flops 60817408 | bytes 4214784 | tf_op jit(solution)/shard_map/while/body/eval_jaxpr/reduce_sum | solution.py:17
  328.1 25.9 %convert_reduce_fusion.3 = bf16[512,4096]{1,0:T(8,128)(2,1)} fusion(s32[10,512]{1,0:T(8,128)S(1)} %bitcast.73), kind=kLoop, calls=%fused_computation.6.clone.1 | loop fusion | flops 60817408 | bytes 4214784 | tf_op jit(solution)/shard_map/while/body/eval_jaxpr/reduce_sum | solution.py:17
  358.2 25.9 %convert_reduce_fusion.3 = bf16[512,4096]{1,0:T(8,128)(2,1)} fusion(s32[10,512]{1,0:T(8,128)S(1)} %bitcast.73), kind=kLoop, calls=%fused_computation.6.clone.1 | loop fusion | flops 60817408 | bytes 4214784 | tf_op jit(solution)/shard_map/while/body/eval_jaxpr/reduce_sum | solution.py:17
  388.3 25.9 %convert_reduce_fusion.3 = bf16[512,4096]{1,0:T(8,128)(2,1)} fusion(s32[10,512]{1,0:T(8,128)S(1)} %bitcast.73), kind=kLoop, calls=%fused_computation.6.clone.1 | loop fusion | flops 60817408 | bytes 4214784 | tf_op jit(solution)/shard_map/while/body/eval_jaxpr/reduce_sum | solution.py:17
  418.3 25.9 %convert_reduce_fusion.3 = bf16[512,4096]{1,0:T(8,128)(2,1)} fusion(s32[10,512]{1,0:T(8,128)S(1)} %bitcast.73), kind=kLoop, calls=%fused_computation.6.clone.1 | loop fusion | flops 60817408 | bytes 4214784 | tf_op jit(solution)/shard_map/while/body/eval_jaxpr/reduce_sum | solution.py:17
  448.4 25.9 %convert_reduce_fusion.3 = bf16[512,4096]{1,0:T(8,128)(2,1)} fusion(s32[10,512]{1,0:T(8,128)S(1)} %bitcast.73), kind=kLoop, calls=%fused_computation.6.clone.1 | loop fusion | flops 60817408 | bytes 4214784 | tf_op jit(solution)/shard_map/while/body/eval_jaxpr/reduce_sum | solution.py:17
  478.5 25.9 %convert_reduce_fusion.3 = bf16[512,4096]{1,0:T(8,128)(2,1)} fusion(s32[10,512]{1,0:T(8,128)S(1)} %bitcast.73), kind=kLoop, calls=%fused_computation.6.clone.1 | loop fusion | flops 60817408 | bytes 4214784 | tf_op jit(solution)/shard_map/while/body/eval_jaxpr/reduce_sum | solution.py:17
  508.6 25.9 %convert_reduce_fusion.3 = bf16[512,4096]{1,0:T(8,128)(2,1)} fusion(s32[10,512]{1,0:T(8,128)S(1)} %bitcast.73), kind=kLoop, calls=%fused_computation.6.clone.1 | loop fusion | flops 60817408 | bytes 4214784 | tf_op jit(solution)/shard_map/while/body/eval_jaxpr/reduce_sum | solution.py:17
  538.7 25.9 %convert_reduce_fusion.3 = bf16[512,4096]{1,0:T(8,128)(2,1)} fusion(s32[10,512]{1,0:T(8,128)S(1)} %bitcast.73), kind=kLoop, calls=%fused_computation.6.clone.1 | loop fusion | flops 60817408 | bytes 4214784 | tf_op jit(solution)/shard_map/while/body/eval_jaxpr/reduce_sum | solution.py:17
  568.7 25.9 %convert_reduce_fusion.3 = bf16[512,4096]{1,0:T(8,128)(2,1)} fusion(s32[10,512]{1,0:T(8,128)S(1)} %bitcast.73), kind=kLoop, calls=%fused_computation.6.clone.1 | loop fusion | flops 60817408 | bytes 4214784 | tf_op jit(solution)/shard_map/while/body/eval_jaxpr/reduce_sum | solution.py:17
  598.8 25.9 %convert_reduce_fusion.3 = bf16[512,4096]{1,0:T(8,128)(2,1)} fusion(s32[10,512]{1,0:T(8,128)S(1)} %bitcast.73), kind=kLoop, calls=%fused_computation.6.clone.1 | loop fusion | flops 60817408 | bytes 4214784 | tf_op jit(solution)/shard_map/while/body/eval_jaxpr/reduce_sum | solution.py:17
  632.8 6.0 fusion.27
  638.8 6.6 multiply_convert_fusion
  646.7 4.4 fusion.23
  654.5 27.5 %fusion.39 = f32[7680,256]{1,0:T(8,128)S(1)} fusion(f32[512,7680]{1,0:T(8,128)S(1)} %bitcast.69, f32[512,256]{1,0:T(8,128)S(1)} %convolution_multiply_fusion), kind=kOutput, calls=%fused_computation.76 | convolution fusion | flops 12079595520 | bytes 24117248 | tf_op jit(solution)/shard_map/dot_general | solution.py:56
  682.3 5.3 fusion.16
  691.8 4.5 gather_fusion.3
  696.9 241.9 %all-reduce.3.cloned.1.call-done = (f32[128,256]{1,0:T(8,128)}, f32[128,256]{1,0:T(8,128)}, f32[256,172]{0,1:T(8,128)}, f32[256,172]{0,1:T(8,128)}) async-done(((f32[128,256]{1,0:T(8,128)}, f32[128,256]{1,0:T(8,128)}, f32[256,172]{0,1:T(8,128)}, f32[256,172]{0,1:T(8,128)}), (f32[128,256]{1,0:T(8,128)}, f32[128,256]{1,0:T(8,128)}, f32[256,172]{0,1:T(8,128)}, ...) | async-done | bytes 614416 | tf_op jit(solution)/shard_map/psum | solution.py:118
  (119 shorter events, 95.0 us)
Async XLA Ops:
  7.2 638.2 %copy-start = (bf16[256,172]{0,1:T(8,128)(2,1)S(1)}, bf16[256,172]{0,1:T(8,128)(2,1)}, u32[]{:S(2)}) copy-start(bf16[256,172]{0,1:T(8,128)(2,1)} %param.28) | copy-start | bytes 264196
  8.6 99.2 %all-to-all-start.2 = ((s32[64,1,32]{2,1,0:T(1,128)}), s32[64,1,32]{2,1,0:T(1,128)S(1)}, u32[]{:S(2)}, u32[]{:S(2)}) async-start(s32[64,1,32]{2,1,0:T(1,128)} %bitcast.5), calls=%async_computation.2 | async-start | bytes 65536 | tf_op jit(solution)/shard_map/all_to_all | solution.py:97
  24.1 83.1 %copy-start.6 = (s32[1,512]{1,0:T(1,128)S(1)}, s32[1,512]{1,0:T(1,128)}, u32[]{:S(2)}) copy-start(s32[1,512]{1,0:T(1,128)} %param.25) | copy-start | bytes 6148
  24.2 83.1 %copy-start.7 = (s32[1,4,512]{2,1,0:T(4,128)S(1)}, s32[1,4,512]{2,1,0:T(4,128)}, u32[]{:S(2)}) copy-start(s32[1,4,512]{2,1,0:T(4,128)} %param.19) | copy-start | bytes 24580
  24.2 107.9 %copy-start.4 = (s32[1,7680]{1,0:T(1,128)S(1)}, s32[1,7680]{1,0:T(1,128)}, u32[]{:S(2)}) copy-start(s32[1,7680]{1,0:T(1,128)} %param.22) | copy-start | bytes 92164
  107.2 47.3 %copy-start.3 = (s32[1,10,7680]{2,0,1:T(1,128)S(1)}, s32[1,10,7680]{2,0,1:T(1,128)}, u32[]{:S(2)}) copy-start(s32[1,10,7680]{2,0,1:T(1,128)} %param.23) | copy-start | bytes 921604
  107.9 13.6 %all-to-all-start = ((s32[4,1,512]{2,1,0:T(1,128)}), s32[4,1,512]{2,1,0:T(1,128)S(1)}, u32[]{:S(2)}, u32[]{:S(2)}) async-start(s32[4,1,512]{2,1,0:T(1,128)} %all_to_all.26), calls=%async_computation | async-start | bytes 16384 | tf_op jit(solution)/shard_map/all_to_all | solution.py:89
  121.5 28.3 %all-to-all-start.3 = ((bf16[64,32,128]{2,1,0:T(8,128)(2,1)}), bf16[64,32,128]{2,1,0:T(8,128)(2,1)S(1)}, u32[]{:S(2)}, u32[]{:S(2)}) async-start(bf16[64,32,128]{2,1,0:T(8,128)(2,1)} %broadcast_select_fusion.3), calls=%async_computation.3 | async-start | bytes 1048576 | tf_op jit(solution)/shard_map/all_to_all | solution.py:94
  149.8 13.4 %all-to-all-start.1 = ((bf16[4,512,128]{2,1,0:T(8,128)(2,1)}), bf16[4,512,128]{2,1,0:T(8,128)(2,1)S(1)}, u32[]{:S(2)}, u32[]{:S(2)}) async-start(bf16[4,512,128]{2,1,0:T(8,128)(2,1)} %broadcast_select_fusion.5), calls=%async_computation.1 | async-start | bytes 1048576 | tf_op jit(solution)/shard_map/all_to_all | solution.py:91
  154.3 784.5 %all-reduce.3.cloned.1.call-start = ((), (), s32[]{:S(2)}) async-start(), calls=%async_computation.4 | async-start | bytes 1245184 | tf_op jit(solution)/shard_map/psum | solution.py:118
  177.7 455.1 %copy-start.5 = (bf16[128,256]{1,0:T(8,128)(2,1)S(1)}, bf16[128,256]{1,0:T(8,128)(2,1)}, u32[]{:S(2)}) copy-start(bf16[128,256]{1,0:T(8,128)(2,1)} %param.26) | copy-start | bytes 196612
  632.7 6.0 copy-start.8
  632.7 13.9 %slice-start = ((s8[15728640]{0:T(1024)(128)(4,1)}), s8[4194304]{0:T(1024)(128)(4,1)S(1)}, s32[]{:S(2)}) async-start(s8[15728640]{0:T(1024)(128)(4,1)} %bitcast.68), calls=%async_computation.5 | async-start | bytes 8388608
  632.8 13.9 %slice-start.1 = ((s8[15728640]{0:T(1024)(128)(4,1)}), s8[4194304]{0:T(1024)(128)(4,1)S(1)}, s32[]{:S(2)}) async-start(s8[15728640]{0:T(1024)(128)(4,1)} %bitcast.68), calls=%async_computation.6 | async-start | bytes 8388608
  638.7 7.9 slice-start.2
  638.8 7.9 slice-start.3
  646.6 4.5 copy-start.2
  682.3 7.9 copy-start.1
Sparse Core Ops, SparseCore 0:
  691.9 246.8 all-reduce.2
where the time goes:
time: 959 us; the launch traced here: 952 us
  other arithmetic  487 us (51%)
  waiting for transfers between devices  257 us (27%)
  matrix products  116 us (12%)
  local copies, waits for them, and re-layouts  45.4 us (5%)
  starting transfers between devices  32.5 us (3%)
  between operations  14.7 us (2%)
    reduce_sum x15, other arithmetic, one_block(): jnp.sum((block_positions[:, :, None] == columns).astype(jnp.float32), axi...  388 us
    psum x1, waiting for transfers between devices, body(): totals = lax.psum((term_a, term_b, term_c, term_d), ('clique', 'group'))  242 us
    reduce_sum x1, other arithmetic, sage_step(): jnp.sum((seed_neigh[:, :, None] == node_index).astype(jnp.float32), axis=0)  83.1 us
    dot_general x15, matrix products, one_block(): jnp.dot(matches.astype(jnp.bfloat16), table, preferred_element_type=jnp.f...  62.3 us
    dot_general x1, matrix products, sage_step(): lax.dot_general(seed_counts, back_second, (((0,), (0,)), ((), ())), preci...  27.5 us
  transfers between devices with their start and end apart: 5, of which 3 were waited for; matrix products, arithmetic and copies ran while one was open for 12% of the time, Pallas kernels for 0%

commit v1 on v0

v1 whole, which is shorter than its diff:
```python
import jax
import jax.numpy as jnp
import numpy as np
from jax import lax
from jax.experimental import pallas as pl
from jax.experimental.pallas import tpu as pltpu
from jax.sharding import Mesh
from jax.sharding import PartitionSpec as P

AXES = ("clique", "z", "y", "core")
GROUP = ("z", "y", "core")
F = 128
HID = 256
CLASSES = 172
CLASS_ROWS = 176
SEEDS = 512
MID = 7680
FAN0 = 10
FAN1 = 15
HOT_ROWS = 2048
COLD_ROWS = 2048
STEP = 128
SLOTS = SEEDS * (FAN1 + 1)
CHUNKS = SLOTS // STEP
SEED_CHUNKS = SEEDS // STEP
TERM_ROWS = 1280
HALF_ROWS = TERM_ROWS // 2
GELU_C = float(np.sqrt(2.0 / np.pi))
GELU_A = 0.044715


def tree_sum(rows):
    while len(rows) > 1:
        rows = [
            rows[i] + rows[i + 1] if i + 1 < len(rows) else rows[i]
            for i in range(0, len(rows), 2)
        ]
    return rows[0]


def train_kernel(
    counts, where_hot, first_slots, nbr1, nbr2, mid_self,
    hot0, hot1, hot2, hot3, cold, labels, w1_self, w1_neigh, w2_self, w2_neigh,
    loss_out, terms_out,
    slots, n0, n1, n2, n3, n4, n5, n6, n7, n8, n9, own, copied,
    table, x_even, x_odd, w1, w2s, w2n, x_all, slope, hidden, hidden_b, grad_logits, back, w1_acc,
):
    neighbours = (n0, n1, n2, n3, n4, n5, n6, n7, n8, n9)
    copies = [pltpu.make_async_copy(nbr1.at[k, 0], neighbours[k], copied.at[k]) for k in range(FAN0)]
    copies.append(pltpu.make_async_copy(mid_self.at[0], own, copied.at[FAN0]))
    copies.append(
        pltpu.make_async_copy(first_slots.at[0], slots.at[pl.ds(0, SEEDS)], copied.at[FAN0 + 1])
    )
    for k in range(FAN1):
        copies.append(
            pltpu.make_async_copy(
                nbr2.at[k, 0],
                slots.at[pl.ds((k + 1) * SEEDS, SEEDS)],
                copied.at[FAN0 + 2 + k],
            )
        )
    copies.append(
        pltpu.make_async_copy(
            first_slots.at[0, pl.ds(0, 128)], slots.at[pl.ds(SLOTS, 128)], copied.at[FAN0 + FAN1 + 2]
        )
    )
    for copy in copies:
        copy.start()

    f32, bf16 = jnp.float32, jnp.bfloat16

    for d, block in enumerate((hot0, hot1, hot2, hot3)):
        start = pl.multiple_of(where_hot[d] * 512, 512)
        table[pl.ds(start, 512), :] = block[...].astype(f32)
    slot_index = lax.broadcasted_iota(jnp.int32, (32, F), 0)

    def place_cold(o, carry):
        rows = cold[o].astype(f32)
        live = slot_index < counts[o]
        table[pl.ds(pl.multiple_of(HOT_ROWS + o * 32, 32), 32), :] = jnp.where(live, rows, 0.0)
        return carry

    lax.fori_loop(0, 64, place_cold, 0, unroll=4)

    w1[0:F, :] = w1_self[...]
    w1[F : 2 * F, :] = w1_neigh[...]
    for padded, given in ((w2s, w2_self), (w2n, w2_neigh)):
        padded[...] = jnp.zeros((256, HID), bf16)
        padded[0:CLASSES, :] = given[...]
    hidden[...] = jnp.zeros((2 * SEEDS, HID), f32)

    def gather(chunk, buffer):
        base = chunk * STEP
        for u in range(STEP):
            m = slots[base + u]
            rows = [table[pl.ds(near[m], 1), :] for near in neighbours]
            buffer[u : u + 1, 0:F] = table[pl.ds(own[m], 1), :]
            buffer[u : u + 1, F : 2 * F] = tree_sum(rows)

    def forward(chunk, buffer):
        row = pl.multiple_of(chunk * STEP, STEP)
        x_all[pl.ds(row, STEP), 0:F] = buffer[:, 0:F].astype(bf16)
        x_all[pl.ds(row, STEP), F : 2 * F] = (buffer[:, F : 2 * F] * (1.0 / FAN0)).astype(bf16)
        x = jnp.concatenate(
            [buffer[:, 0:F].astype(bf16), (buffer[:, F : 2 * F] * (1.0 / FAN0)).astype(bf16)], axis=1
        )
        v = jnp.dot(x, w1[...], preferred_element_type=f32)
        square = v * v
        t = jnp.tanh(v * (GELU_C + (GELU_C * GELU_A) * square))
        half = 0.5 + 0.5 * t
        h = (v * half).astype(bf16).astype(f32)
        slope[pl.ds(row, STEP), :] = half + (0.5 * v) * (1.0 - t * t) * (
            GELU_C + (3.0 * GELU_C * GELU_A) * square
        )
        into = pl.multiple_of(
            lax.rem(chunk, SEED_CHUNKS) * STEP + jnp.where(chunk >= SEED_CHUNKS, SEEDS, 0), STEP
        )
        hidden[pl.ds(into, STEP), :] += h

    for copy in copies:
        copy.wait()
    gather(0, x_even)

    def two_chunks(i, carry):
        gather(2 * i + 1, x_odd)
        forward(2 * i, x_even)
        gather(2 * i + 2, x_even)
        forward(2 * i + 1, x_odd)
        return carry

    lax.fori_loop(0, CHUNKS // 2, two_chunks, 0)

    hidden_b[0:SEEDS, :] = hidden[0:SEEDS, :].astype(bf16)
    hidden_b[SEEDS:, :] = (hidden[SEEDS:, :] / FAN1).astype(bf16)
    nt = (((1,), (1,)), ((), ()))
    tn = (((0,), (0,)), ((), ()))
    eye = lax.broadcasted_iota(jnp.int32, (128, 128), 0) == lax.broadcasted_iota(
        jnp.int32, (128, 128), 1
    )
    lane = lax.broadcasted_iota(jnp.int32, (128, 256), 1)
    for b in range(SEEDS // 128):
        rows = slice(b * 128, (b + 1) * 128)
        logits = lax.dot_general(
            hidden_b[rows, :], w2s[...], nt, preferred_element_type=f32
        ) + lax.dot_general(
            hidden_b[SEEDS + b * 128 : SEEDS + (b + 1) * 128, :], w2n[...], nt,
            preferred_element_type=f32,
        )
        label_row = labels[:, rows].astype(f32)
        label = jnp.sum(jnp.where(eye, label_row, 0.0), axis=1, keepdims=True).astype(jnp.int32)
        valid = lane < CLASSES
        top = jnp.max(jnp.where(valid, logits, -3.0e38), axis=1, keepdims=True)
        total = jnp.sum(jnp.where(valid, jnp.exp(logits - top), 0.0), axis=1, keepdims=True)
        log_total = jnp.log(total) + top
        hit = lane == label
        picked = jnp.sum(jnp.where(hit, logits, 0.0), axis=1, keepdims=True)
        loss = log_total - picked
        loss_out[:, rows] = jnp.sum(jnp.where(eye, loss, 0.0), axis=0, keepdims=True)
        probs = jnp.where(valid, jnp.exp(logits - log_total), 0.0)
        grad_logits[rows, :] = ((probs - hit.astype(f32)) / SEEDS).astype(bf16)

    g = grad_logits[...]
    terms_out[608:HALF_ROWS, :] = jnp.zeros((HALF_ROWS - 608, F), f32)
    terms_out[HALF_ROWS + 608 :, :] = jnp.zeros((HALF_ROWS - 608, F), f32)
    for at, part in ((256, slice(0, SEEDS)), (256 + CLASS_ROWS, slice(SEEDS, 2 * SEEDS))):
        term = lax.dot_general(g, hidden_b[part, :], tn, preferred_element_type=f32)
        terms_out[at : at + CLASS_ROWS, :] = term[0:CLASS_ROWS, 0:F]
        terms_out[HALF_ROWS + at : HALF_ROWS + at + CLASS_ROWS, :] = term[0:CLASS_ROWS, F:]
    back[0:SEEDS, :] = jnp.dot(g, w2s[...], preferred_element_type=f32)
    back[SEEDS:, :] = jnp.dot(g, w2n[...], preferred_element_type=f32) / FAN1

    def backward(j, into):
        row = pl.multiple_of(j * SEEDS, SEEDS)
        grad_pre = (slope[pl.ds(row, SEEDS), :] * back[into, :]).astype(bf16)
        return lax.dot_general(x_all[pl.ds(row, SEEDS), :], grad_pre, tn, preferred_element_type=f32)

    w1_acc[...] = backward(0, slice(0, SEEDS))

    def add_block(j, carry):
        w1_acc[...] += backward(j, slice(SEEDS, 2 * SEEDS))
        return carry

    lax.fori_loop(1, FAN1 + 1, add_block, 0)
    terms_out[0:256, :] = w1_acc[:, 0:F]
    terms_out[HALF_ROWS : HALF_ROWS + 256, :] = w1_acc[:, F:]


def train(counts, where_hot, nbr1, nbr2, mid_self, hot, cold, labels, w1_self, w1_neigh, w2_self_t, w2_neigh_t):
    smem = pl.BlockSpec(memory_space=pltpu.SMEM)
    vmem = pl.BlockSpec(memory_space=pltpu.VMEM)
    anywhere = pl.BlockSpec(memory_space=pl.ANY)
    first_slots = np.arange(SEEDS, dtype=np.int32)[None]
    return pl.pallas_call(
        train_kernel,
        out_shape=(
            jax.ShapeDtypeStruct((1, SEEDS), jnp.float32),
            jax.ShapeDtypeStruct((TERM_ROWS, F), jnp.float32),
        ),
        in_specs=[smem] * 2 + [anywhere] * 4 + [vmem] * 10,
        out_specs=(vmem, vmem),
        scratch_shapes=[
            pltpu.SMEM((SLOTS + 128,), jnp.int32),
            *[pltpu.SMEM((MID,), jnp.int32) for _ in range(FAN0 + 1)],
            pltpu.SemaphoreType.DMA((FAN0 + FAN1 + 3,)),
            pltpu.VMEM((HOT_ROWS + COLD_ROWS, F), jnp.float32),
            pltpu.VMEM((STEP, 2 * F), jnp.float32),
            pltpu.VMEM((STEP, 2 * F), jnp.float32),
            pltpu.VMEM((2 * F, HID), jnp.bfloat16),
            pltpu.VMEM((256, HID), jnp.bfloat16),
            pltpu.VMEM((256, HID), jnp.bfloat16),
            pltpu.VMEM((SLOTS, 2 * F), jnp.bfloat16),
            pltpu.VMEM((SLOTS, HID), jnp.float32),
            pltpu.VMEM((2 * SEEDS, HID), jnp.float32),
            pltpu.VMEM((2 * SEEDS, HID), jnp.bfloat16),
            pltpu.VMEM((SEEDS, 256), jnp.bfloat16),
            pltpu.VMEM((2 * SEEDS, HID), jnp.float32),
            pltpu.VMEM((2 * F, HID), jnp.float32),
        ],
        compiler_params=pltpu.CompilerParams(vmem_limit_bytes=44 << 20),
        cost_estimate=pl.CostEstimate(flops=4 << 30, bytes_accessed=4 << 20, transcendentals=2 << 20),
        name="train",
    )(
        counts, where_hot, jnp.asarray(first_slots), nbr1[:, None], nbr2[:, None], mid_self[None],
        *hot, cold, labels, w1_self, w1_neigh, w2_self_t, w2_neigh_t,
    )


def swap_hot(hot_shard, hot_ids):
    me = lax.axis_index("clique")
    peers = [lax.rem(me + d, 4) for d in range(4)]
    asked = [lax.dynamic_index_in_dim(hot_ids, peer, 0, keepdims=False) for peer in peers]
    requests = [asked[0]] + [
        lax.ppermute(asked[d], "clique", [(i, (i + d) % 4) for i in range(4)]) for d in (1, 2, 3)
    ]
    return peers, requests


def serve_hot(hot_shard, requests):
    rows = [hot_shard.at[ids].get(mode="promise_in_bounds") for ids in requests]
    return [rows[0]] + [
        lax.ppermute(rows[d], "clique", [(i, (i - d) % 4) for i in range(4)]) for d in (1, 2, 3)
    ]


def exchange(x, axes):
    return lax.all_to_all(x, axes, split_axis=0, concat_axis=0, tiled=True)


def share(x, axes, n):
    return exchange(jnp.broadcast_to(x[None], (n,) + x.shape), axes)


SWAP = [(0, 1), (1, 0)]


def sum_everywhere(x):
    tiles = x.reshape(TERM_ROWS // 8, 8, F)
    half = tiles.shape[0] // 2
    core = lax.axis_index("core")
    theirs = lax.dynamic_slice_in_dim(tiles, (1 - core) * half, half, 0)
    mine = lax.dynamic_slice_in_dim(tiles, core * half, half, 0)
    mine = mine + lax.ppermute(theirs, "core", SWAP)
    mine = exchange(mine.reshape(16, half // 16, 8, F), ("clique", "y")).sum(0)
    mine = share(mine, "z", 8).sum(0)
    mine = share(mine, ("clique", "y"), 16).reshape(half * 8, F)
    other = lax.ppermute(mine, "core", SWAP)
    return jnp.where(core == 0, mine, other), jnp.where(core == 0, other, mine)


def body(
    hot_shard, cold_shard, hot_ids, cold_ids, cold_counts, mid_self, nbr1, nbr2, labels,
    w1_self, w1_neigh, w2_self, w2_neigh,
):
    peers, requests = swap_hot(hot_shard, hot_ids[0])
    asked = exchange(cold_ids[0], GROUP)
    served = cold_shard.at[asked].get(mode="promise_in_bounds")
    cold = exchange(served, GROUP)
    hot = serve_hot(hot_shard, requests)
    loss, terms = train(
        cold_counts[0], jnp.stack(peers).astype(jnp.int32), nbr1[0], nbr2[0], mid_self[0],
        hot, cold, labels, w1_self, w1_neigh, w2_self.T, w2_neigh.T,
    )
    left, right = sum_everywhere(terms)

    def rows(at, n):
        return jnp.concatenate([left[at : at + n], right[at : at + n]], axis=1)

    return (
        loss,
        rows(0, F),
        rows(F, F),
        rows(2 * F, CLASSES).T,
        rows(2 * F + CLASS_ROWS, CLASSES).T,
    )


def solution(mesh):
    mesh = Mesh(mesh.devices.reshape(4, 8, 4, 2), AXES)
    each = P(AXES)
    return jax.shard_map(
        body,
        mesh=mesh,
        in_specs=(P("clique"), P(GROUP)) + (each,) * 7 + (P(),) * 4,
        out_specs=(each, P(), P(), P(), P()),
        check_vma=False,
    )
```

time: 959 us -> 189 us (0.20)
  other arithmetic: 487 us -> 3.66 us
  waiting for transfers between devices: 257 us -> 6.7 us
  matrix products: 116 us -> 0 us
  Pallas kernels: 0 us -> 75.4 us
  blocking collectives: 0 us -> 39.7 us
  local copies, waits for them, and re-layouts: 45.4 us -> 28.1 us
  between operations: 14.7 us -> 0.99 us
    reduce_sum x16 -> x2, other arithmetic: 471 us -> 0.04 us  [the longest x1 0.02 us: sum_everywhere(): mine = exchange(mine.reshape(16, half // 16, 8, F), ('clique', 'y')).sum(0)]
    psum x1 -> x0, waiting for transfers between devices: 242 us -> none  [body(): totals = lax.psum((term_a, term_b, term_c, term_d), ('clique', 'group'))]
    dot_general x27 -> x0, matrix products: 116 us -> none  [the longest x15 62.3 us: one_block(): jnp.dot(matches.astype(jnp.bfloat16), table, preferred_element_type=jnp.f...]
    pallas_call x0 -> x1, Pallas kernels: none -> 75.4 us  [train(): pl.pallas_call(train_kernel, out_shape=(jax.ShapeDtypeStruct((1, SEEDS),...]
    all_to_all x0 -> x3, blocking collectives: none -> 39.7 us  [exchange(): return lax.all_to_all(x, axes, split_axis=0, concat_axis=0, tiled=True)]
    ppermute x0 -> x8, starting transfers between devices: none -> 13.9 us  [the longest x1 4.32 us: sum_everywhere(): other = lax.ppermute(mine, 'core', SWAP)]
    all_to_all x4 -> x2, starting transfers between devices: 32.3 us -> 20.1 us  [exchange(): return lax.all_to_all(x, axes, split_axis=0, concat_axis=0, tiled=True)]
    all_to_all x4 -> x2, waiting for transfers between devices: 15.4 us -> 4.17 us  [exchange(): return lax.all_to_all(x, axes, split_axis=0, concat_axis=0, tiled=True)]
  transfers between devices with their start and end apart: 5 -> 10, of which waited for: 3 -> 3; matrix products, arithmetic and copies ran while one was open for 12% -> 15% of each run, Pallas kernels for 0% -> 0%
where the time goes in v1:
time: 189 us
  Pallas kernels  75.4 us (40%)
  blocking collectives  39.7 us (21%)
  starting transfers between devices  34 us (18%)
  local copies, waits for them, and re-layouts  28.1 us (15%)
  waiting for transfers between devices  6.7 us (4%)
  other arithmetic  3.66 us (2%)
    pallas_call x1, Pallas kernels, train(): pl.pallas_call(train_kernel, out_shape=(jax.ShapeDtypeStruct((1, SEEDS),...  75.4 us
    all_to_all x3, blocking collectives, exchange(): return lax.all_to_all(x, axes, split_axis=0, concat_axis=0, tiled=True)  39.7 us
    all_to_all x2, starting transfers between devices, exchange(): return lax.all_to_all(x, axes, split_axis=0, concat_axis=0, tiled=True)  20.1 us
    gather x4, local copies, waits for them, and re-layouts, serve_hot(): rows = [hot_shard.at[ids].get(mode='promise_in_bounds') for ids in requests]  15.1 us
    gather x1, local copies, waits for them, and re-layouts, body(): served = cold_shard.at[asked].get(mode='promise_in_bounds')  10.5 us
    ppermute x1, starting transfers between devices, sum_everywhere(): other = lax.ppermute(mine, 'core', SWAP)  4.32 us
    ppermute x3, starting transfers between devices, swap_hot(): lax.ppermute(asked[d], 'clique', [(i, (i + d) % 4) for i in range(4)])  4.28 us
    all_to_all x2, waiting for transfers between devices, exchange(): return lax.all_to_all(x, axes, split_axis=0, concat_axis=0, tiled=True)  4.17 us
  transfers between devices with their start and end apart: 10, of which 3 were waited for; matrix products, arithmetic and copies ran while one was open for 15% of the time, Pallas kernels for 0%

profile of v1, /device:TPU:1, one launch (start us, length us, event | category | flops | bytes accessed | tf_op | source)
XLA Modules:
  0.0 188.5 jit_solution(12106061287150457415)
XLA Ops:
  0.6 1.4 copy.21
  2.0 13.2 %all-to-all-start = ((s32[64,1,32]{2,1,0:T(1,128)}), s32[64,1,32]{2,1,0:T(1,128)S(1)}, u32[]{:S(2)}, u32[]{:S(2)}) async-start(s32[64,1,32]{2,1,0:T(1,128)} %bitcast.12), calls=%async_computation | async-start | bytes 65536 | tf_op jit(solution)/shard_map/all_to_all | solution.py:246
  15.2 0.8 constant_dynamic-slice_fusion.1
  16.1 2.8 %collective-permute-start.2 = (s32[512]{0:T(512)S(1)}, s32[512]{0:T(512)S(1)}, u32[]{:S(2)}, u32[]{:S(2)}) collective-permute-start(s32[512]{0:T(512)S(1)} %bitcast.42), channel_id=1, source_target_pairs={{0,128},{64,192},{128,0},{192,64},{1,129},{65,193},{129,1},{193,65... | collective-permute-start | bytes 6152 | tf_op jit(solution)/shard_map/ppermute | solution.py:233
  18.9 0.9 collective-permute-start.4
  19.7 0.6 collective-permute-start
  20.3 4.2 %all-to-all-done = s32[64,1,32]{2,1,0:T(1,128)S(1)} async-done(((s32[64,1,32]{2,1,0:T(1,128)}), s32[64,1,32]{2,1,0:T(1,128)S(1)}, u32[]{:S(2)}, u32[]{:S(2)}) %all-to-all-start) | async-done | bytes 8224 | tf_op jit(solution)/shard_map/all_to_all | solution.py:246
  24.5 0.1 reshape.125
  24.7 0.0 copy-start.9
  24.7 10.5 %gather_fusion.4 = bf16[2048,128]{1,0:T(8,128)(2,1)} fusion(bf16[16384,128]{1,0:T(8,128)(2,1)} %param.15, s32[2048]{0:T(1024)S(1)} %broadcast_clamp_fusion), kind=kCustom, calls=%fused_computation.4 | custom fusion | bytes 1056768 | tf_op jit(solution)/shard_map/gather | solution.py:276
  35.2 7.0 %all-to-all-start.1 = ((bf16[64,32,128]{2,1,0:T(8,128)(2,1)}), bf16[64,32,128]{2,1,0:T(8,128)(2,1)S(1)}, u32[]{:S(2)}, u32[]{:S(2)}) async-start(bf16[64,32,128]{2,1,0:T(8,128)(2,1)} %bitcast.14), calls=%async_computation.1 | async-start | bytes 1048576 | tf_op jit(solution)/shard_map/all_to_all | solution.py:246
  42.2 0.7 compare_select_fusion.1
  43.0 3.8 %gather_fusion.2 = bf16[512,128]{1,0:T(8,128)(2,1)S(1)} fusion(bf16[16384,128]{1,0:T(8,128)(2,1)} %param.14, s32[1024]{0:T(1024)S(1)} %pad_clamp_fusion.1), kind=kCustom, calls=%fused_computation.2 | custom fusion | bytes 264192 | tf_op jit(solution)/shard_map/gather | solution.py:239
  46.8 0.6 collective-permute-start.3
  47.4 3.8 %gather_fusion.3 = bf16[512,128]{1,0:T(8,128)(2,1)S(1)} fusion(bf16[16384,128]{1,0:T(8,128)(2,1)} %param.14, s32[1024]{0:T(1024)S(1)} %pad_clamp_fusion), kind=kCustom, calls=%fused_computation.3 | custom fusion | bytes 264192 | tf_op jit(solution)/shard_map/gather | solution.py:239
  51.2 2.2 %collective-permute-start.5 = (bf16[512,128]{1,0:T(8,128)(2,1)S(1)}, bf16[512,128]{1,0:T(8,128)(2,1)S(1)}, u32[]{:S(2)}, u32[]{:S(2)}) collective-permute-start(bf16[512,128]{1,0:T(8,128)(2,1)S(1)} %gather_fusion.3), channel_id=1, source_target_pairs={{0,64},{64,128},{128,192},{192,0},{1,65},{65,129},{129,193},{193,1... | collective-permute-start | bytes 393224 | tf_op jit(solution)/shard_map/ppermute | solution.py:241
  53.4 3.8 %gather_fusion.1 = bf16[512,128]{1,0:T(8,128)(2,1)S(1)} fusion(bf16[16384,128]{1,0:T(8,128)(2,1)} %param.14, s32[1024]{0:T(1024)S(1)} %pad_clamp_fusion.2), kind=kCustom, calls=%fused_computation.1 | custom fusion | bytes 264192 | tf_op jit(solution)/shard_map/gather | solution.py:239
  57.2 0.8 collective-permute-start.1
  58.0 3.8 %gather_fusion = bf16[512,128]{1,0:T(8,128)(2,1)S(1)} fusion(bf16[16384,128]{1,0:T(8,128)(2,1)} %param.14, s32[1024]{0:T(1024)S(1)} %pad_clamp_fusion.3), kind=kCustom, calls=%fused_computation | custom fusion | bytes 264192 | tf_op jit(solution)/shard_map/gather | solution.py:239
  61.8 0.1 pad_add_fusion.where_hot
  62.0 75.4 %train.1 = (f32[1,512]{1,0:T(1,128)}, f32[1280,128]{1,0:T(8,128)S(1)}) custom-call(s32[64]{0:T(128)S(1)} %bitcast.35, s32[4]{0:T(128)S(1)} %pad_add_fusion.where_hot, s32[1,512]{1,0:T(1,128)S(1)} %copy-done.9, s32[10,1,7680]{2,1,0:T(1,128)S(1)} %bitcast.31, s32[15,1,512]{2,1,0:T(1,128)S(1)} %bitcast.34, s32[1,7680]{1,0:T(1,128)S(1)} %copy-done.6, ...), custom_call_target="tpu_custom_call" | custom-call | flops 4294967296 | bytes 4194304 | tf_op jit(solution)/shard_map/train/pallas_call | solution.py:193
  137.4 1.6 collective-permute-start.6
  139.0 1.3 collective-permute-done.6
  140.3 13.4 %all_to_all.32 = f32[16,5,8,128]{3,2,1,0:T(8,128)S(1)} all-to-all(f32[16,5,8,128]{3,2,1,0:T(8,128)S(1)} %bitcast.36), channel_id=1, replica_groups=mesh['clique'=4,'z'=8,'y'=4,'core'=2] {'clique','y'}, dimensions={0} | all-to-all | bytes 655360 | tf_op jit(solution)/shard_map/all_to_all | solution.py:246
  153.8 14.8 %all_to_all.33 = f32[8,5,8,128]{3,2,1,0:T(8,128)S(1)} all-to-all(f32[8,5,8,128]{3,2,1,0:T(8,128)S(1)} %broadcast_in_dim.26), channel_id=1, replica_groups=mesh['clique'=4,'z'=8,'y'=4,'core'=2] {'z'}, dimensions={0} | all-to-all | bytes 327680 | tf_op jit(solution)/shard_map/all_to_all | solution.py:246
  168.6 11.5 %all_to_all.34 = f32[16,5,8,128]{3,2,1,0:T(8,128)S(1)} all-to-all(f32[16,5,8,128]{3,2,1,0:T(8,128)S(1)} %broadcast_in_dim.27), channel_id=1, replica_groups=mesh['clique'=4,'z'=8,'y'=4,'core'=2] {'clique','y'}, dimensions={0} | all-to-all | bytes 655360 | tf_op jit(solution)/shard_map/all_to_all | solution.py:246
  180.1 4.3 %collective-permute-start.7 = (f32[640,128]{1,0:T(8,128)S(1)}, f32[640,128]{1,0:T(8,128)S(1)}, u32[]{:S(2)}, u32[]{:S(2)}) collective-permute-start(f32[640,128]{1,0:T(8,128)S(1)} %bitcast.37), channel_id=1, source_target_pairs={{0,1},{1,0},{2,3},{3,2},{4,5},{5,4},{6,7},{7,6},{8,9},{9,8},{10,11... | collective-permute-start | bytes 983048 | tf_op jit(solution)/shard_map/ppermute | solution.py:266
  184.4 1.3 collective-permute-done.7
  185.8 0.7 maximum_bitcast_fusion.1
  186.5 0.7 maximum_bitcast_fusion
  187.2 0.7 pad_maximum_fusion.1
  187.8 0.7 pad_maximum_fusion
  (45 shorter events, 0.4 us)
Async XLA Ops:
  2.0 22.5 %all-to-all-start = ((s32[64,1,32]{2,1,0:T(1,128)}), s32[64,1,32]{2,1,0:T(1,128)S(1)}, u32[]{:S(2)}, u32[]{:S(2)}) async-start(s32[64,1,32]{2,1,0:T(1,128)} %bitcast.12), calls=%async_computation | async-start | bytes 65536 | tf_op jit(solution)/shard_map/all_to_all | solution.py:246
  16.1 26.9 %collective-permute-start.2 = (s32[512]{0:T(512)S(1)}, s32[512]{0:T(512)S(1)}, u32[]{:S(2)}, u32[]{:S(2)}) collective-permute-start(s32[512]{0:T(512)S(1)} %bitcast.42), channel_id=1, source_target_pairs={{0,128},{64,192},{128,0},{192,64},{1,129},{65,193},{129,1},{193,65... | collective-permute-start | bytes 6152 | tf_op jit(solution)/shard_map/ppermute | solution.py:233
  18.9 24.1 %collective-permute-start.4 = (s32[512]{0:T(512)S(1)}, s32[512]{0:T(512)S(1)}, u32[]{:S(2)}, u32[]{:S(2)}) collective-permute-start(s32[512]{0:T(512)S(1)} %bitcast.41), channel_id=1, source_target_pairs={{0,192},{64,0},{128,64},{192,128},{1,193},{65,1},{129,65},{193,129... | collective-permute-start | bytes 6152 | tf_op jit(solution)/shard_map/ppermute | solution.py:233
  19.7 33.6 %collective-permute-start = (s32[512]{0:T(512)S(1)}, s32[512]{0:T(512)S(1)}, u32[]{:S(2)}, u32[]{:S(2)}) collective-permute-start(s32[512]{0:T(512)S(1)} %bitcast.40), channel_id=1, source_target_pairs={{0,64},{64,128},{128,192},{192,0},{1,65},{65,129},{129,193},{193,1... | collective-permute-start | bytes 6152 | tf_op jit(solution)/shard_map/ppermute | solution.py:233
  24.6 37.3 %copy-start = (s32[1,10,7680]{2,0,1:T(1,128)S(1)}, s32[1,10,7680]{2,0,1:T(1,128)}, u32[]{:S(2)}) copy-start(s32[1,10,7680]{2,0,1:T(1,128)} %param.20) | copy-start | bytes 921604
  24.6 37.3 %copy-start.1 = (bf16[256,172]{0,1:T(8,128)(2,1)S(1)}, bf16[256,172]{0,1:T(8,128)(2,1)}, u32[]{:S(2)}) copy-start(bf16[256,172]{0,1:T(8,128)(2,1)} %param.25) | copy-start | bytes 264196
  24.6 37.3 %copy-start.2 = (bf16[256,172]{0,1:T(8,128)(2,1)S(1)}, bf16[256,172]{0,1:T(8,128)(2,1)}, u32[]{:S(2)}) copy-start(bf16[256,172]{0,1:T(8,128)(2,1)} %param.26) | copy-start | bytes 264196
  24.6 37.3 %copy-start.3 = (bf16[128,256]{1,0:T(8,128)(2,1)S(1)}, bf16[128,256]{1,0:T(8,128)(2,1)}, u32[]{:S(2)}) copy-start(bf16[128,256]{1,0:T(8,128)(2,1)} %w1_self.1) | copy-start | bytes 196612
  24.6 37.3 %copy-start.4 = (bf16[128,256]{1,0:T(8,128)(2,1)S(1)}, bf16[128,256]{1,0:T(8,128)(2,1)}, u32[]{:S(2)}) copy-start(bf16[128,256]{1,0:T(8,128)(2,1)} %w1_neigh.1) | copy-start | bytes 196612
  24.7 37.3 %copy-start.5 = (s32[1,15,512]{2,0,1:T(1,128)S(1)}, s32[1,15,512]{2,0,1:T(1,128)}, u32[]{:S(2)}) copy-start(s32[1,15,512]{2,0,1:T(1,128)} %param.21) | copy-start | bytes 92164
  24.7 37.3 %copy-start.6 = (s32[1,7680]{1,0:T(1,128)S(1)}, s32[1,7680]{1,0:T(1,128)}, u32[]{:S(2)}) copy-start(s32[1,7680]{1,0:T(1,128)} %mid_self.1) | copy-start | bytes 92164
  24.7 37.3 %copy-start.7 = (s32[1,512]{1,0:T(1,128)S(1)}, s32[1,512]{1,0:T(1,128)}, u32[]{:S(2)}) copy-start(s32[1,512]{1,0:T(1,128)} %labels.1) | copy-start | bytes 6148
  24.7 37.3 %copy-start.8 = (s32[1,64]{1,0:T(1,128)S(1)}, s32[1,64]{1,0:T(1,128)}, u32[]{:S(2)}) copy-start(s32[1,64]{1,0:T(1,128)} %param.18) | copy-start | bytes 772
  24.7 37.3 %copy-start.9 = (s32[1,512]{1,0:T(1,128)S(1)}, s32[1,512]{1,0:T(1,128)}, u32[]{:S(2)}) copy-start(s32[1,512]{1,0:T(1,128)} %constant.55.clone.first_slots) | copy-start | bytes 6148
  35.2 26.6 %all-to-all-start.1 = ((bf16[64,32,128]{2,1,0:T(8,128)(2,1)}), bf16[64,32,128]{2,1,0:T(8,128)(2,1)S(1)}, u32[]{:S(2)}, u32[]{:S(2)}) async-start(bf16[64,32,128]{2,1,0:T(8,128)(2,1)} %bitcast.14), calls=%async_computation.1 | async-start | bytes 1048576 | tf_op jit(solution)/shard_map/all_to_all | solution.py:246
  46.8 15.1 %collective-permute-start.3 = (bf16[512,128]{1,0:T(8,128)(2,1)S(1)}, bf16[512,128]{1,0:T(8,128)(2,1)S(1)}, u32[]{:S(2)}, u32[]{:S(2)}) collective-permute-start(bf16[512,128]{1,0:T(8,128)(2,1)S(1)} %gather_fusion.2), channel_id=1, source_target_pairs={{0,128},{64,192},{128,0},{192,64},{1,129},{65,193},{129,1},{193,65... | collective-permute-start | bytes 393224 | tf_op jit(solution)/shard_map/ppermute | solution.py:241
  51.2 10.7 %collective-permute-start.5 = (bf16[512,128]{1,0:T(8,128)(2,1)S(1)}, bf16[512,128]{1,0:T(8,128)(2,1)S(1)}, u32[]{:S(2)}, u32[]{:S(2)}) collective-permute-start(bf16[512,128]{1,0:T(8,128)(2,1)S(1)} %gather_fusion.3), channel_id=1, source_target_pairs={{0,64},{64,128},{128,192},{192,0},{1,65},{65,129},{129,193},{193,1... | collective-permute-start | bytes 393224 | tf_op jit(solution)/shard_map/ppermute | solution.py:241
  57.2 4.7 %collective-permute-start.1 = (bf16[512,128]{1,0:T(8,128)(2,1)S(1)}, bf16[512,128]{1,0:T(8,128)(2,1)S(1)}, u32[]{:S(2)}, u32[]{:S(2)}) collective-permute-start(bf16[512,128]{1,0:T(8,128)(2,1)S(1)} %gather_fusion.1), channel_id=1, source_target_pairs={{0,192},{64,0},{128,64},{192,128},{1,193},{65,1},{129,65},{193,129... | collective-permute-start | bytes 393224 | tf_op jit(solution)/shard_map/ppermute | solution.py:241
  137.4 2.9 %collective-permute-start.6 = (f32[80,8,128]{2,1,0:T(8,128)S(1)}, f32[80,8,128]{2,1,0:T(8,128)S(1)}, u32[]{:S(2)}, u32[]{:S(2)}) collective-permute-start(f32[80,8,128]{2,1,0:T(8,128)S(1)} %constant_dynamic-slice_fusion), channel_id=1, source_target_pairs={{0,1},{1,0},{2,3},{3,2},{4,5},{5,4},{6,7},{7,6},{8,9},{9,8},{10,11... | collective-permute-start | bytes 983048 | tf_op jit(solution)/shard_map/ppermute | solution.py:262
  180.1 5.6 %collective-permute-start.7 = (f32[640,128]{1,0:T(8,128)S(1)}, f32[640,128]{1,0:T(8,128)S(1)}, u32[]{:S(2)}, u32[]{:S(2)}) collective-permute-start(f32[640,128]{1,0:T(8,128)S(1)} %bitcast.37), channel_id=1, source_target_pairs={{0,1},{1,0},{2,3},{3,2},{4,5},{5,4},{6,7},{7,6},{8,9},{9,8},{10,11... | collective-permute-start | bytes 983048 | tf_op jit(solution)/shard_map/ppermute | solution.py:266

commit v2 on v1

--- a/solution.py
+++ b/solution.py
@@ -23,8 +23,8 @@
 SLOTS = SEEDS * (FAN1 + 1)
 CHUNKS = SLOTS // STEP
 SEED_CHUNKS = SEEDS // STEP
-TERM_ROWS = 1280
-HALF_ROWS = TERM_ROWS // 2
+HALF_ROWS = 640
+PARTS = 8
 GELU_C = float(np.sqrt(2.0 / np.pi))
 GELU_A = 0.044715
 
@@ -39,35 +39,29 @@
 
 
 def train_kernel(
-    counts, where_hot, first_slots, nbr1, nbr2, mid_self,
+    counts, where_hot, core, first_slots, nbr1, nbr2, mid_self,
     hot0, hot1, hot2, hot3, cold, labels, w1_self, w1_neigh, w2_self, w2_neigh,
-    loss_out, terms_out,
+    loss_out, keep_out, send_out,
     slots, n0, n1, n2, n3, n4, n5, n6, n7, n8, n9, own, copied,
-    table, x_even, x_odd, w1, w2s, w2n, x_all, slope, hidden, hidden_b, grad_logits, back, w1_acc,
+    table, x_even, x_odd, w1, w2s, w2n, x_all, slope, hidden, hidden_b, grad_logits, back, w1_acc, terms,
 ):
+    f32, bf16 = jnp.float32, jnp.bfloat16
     neighbours = (n0, n1, n2, n3, n4, n5, n6, n7, n8, n9)
-    copies = [pltpu.make_async_copy(nbr1.at[k, 0], neighbours[k], copied.at[k]) for k in range(FAN0)]
-    copies.append(pltpu.make_async_copy(mid_self.at[0], own, copied.at[FAN0]))
-    copies.append(
-        pltpu.make_async_copy(first_slots.at[0], slots.at[pl.ds(0, SEEDS)], copied.at[FAN0 + 1])
-    )
+    head, tail = pl.ds(0, SEEDS), pl.ds(SEEDS, MID - SEEDS)
+    early, late = [], []
+    for k in range(FAN0):
+        early.append((nbr1.at[k, 0, head], neighbours[k].at[head]))
+        late.append((nbr1.at[k, 0, tail], neighbours[k].at[tail]))
+    early.append((mid_self.at[0, head], own.at[head]))
+    late.append((mid_self.at[0, tail], own.at[tail]))
+    early.append((first_slots.at[0], slots.at[head]))
+    late.append((first_slots.at[0, pl.ds(0, STEP)], slots.at[pl.ds(SLOTS, STEP)]))
     for k in range(FAN1):
-        copies.append(
-            pltpu.make_async_copy(
-                nbr2.at[k, 0],
-                slots.at[pl.ds((k + 1) * SEEDS, SEEDS)],
-                copied.at[FAN0 + 2 + k],
-            )
-        )
-    copies.append(
-        pltpu.make_async_copy(
-            first_slots.at[0, pl.ds(0, 128)], slots.at[pl.ds(SLOTS, 128)], copied.at[FAN0 + FAN1 + 2]
-        )
-    )
-    for copy in copies:
+        late.append((nbr2.at[k, 0], slots.at[pl.ds((k + 1) * SEEDS, SEEDS)]))
+    early = [pltpu.make_async_copy(*pair, copied.at[i]) for i, pair in enumerate(early)]
+    late = [pltpu.make_async_copy(*pair, copied.at[len(early) + i]) for i, pair in enumerate(late)]
+    for copy in early + late:
         copy.start()
-
-    f32, bf16 = jnp.float32, jnp.bfloat16
 
     for d, block in enumerate((hot0, hot1, hot2, hot3)):
         start = pl.multiple_of(where_hot[d] * 512, 512)
@@ -117,11 +111,16 @@
         )
         hidden[pl.ds(into, STEP), :] += h
 
-    for copy in copies:
+    for copy in early:
         copy.wait()
     gather(0, x_even)
 
     def two_chunks(i, carry):
+        @pl.when(i == SEED_CHUNKS // 2 - 1)
+        def _():
+            for copy in late:
+                copy.wait()
+
         gather(2 * i + 1, x_odd)
         forward(2 * i, x_even)
         gather(2 * i + 2, x_even)
@@ -159,13 +158,13 @@
         probs = jnp.where(valid, jnp.exp(logits - log_total), 0.0)
         grad_logits[rows, :] = ((probs - hit.astype(f32)) / SEEDS).astype(bf16)
 
+    left, right = core[0], 1 - core[0]
     g = grad_logits[...]
-    terms_out[608:HALF_ROWS, :] = jnp.zeros((HALF_ROWS - 608, F), f32)
-    terms_out[HALF_ROWS + 608 :, :] = jnp.zeros((HALF_ROWS - 608, F), f32)
+    terms[:, 608:, :] = jnp.zeros((2, HALF_ROWS - 608, F), f32)
     for at, part in ((256, slice(0, SEEDS)), (256 + CLASS_ROWS, slice(SEEDS, 2 * SEEDS))):
         term = lax.dot_general(g, hidden_b[part, :], tn, preferred_element_type=f32)
-        terms_out[at : at + CLASS_ROWS, :] = term[0:CLASS_ROWS, 0:F]
-        terms_out[HALF_ROWS + at : HALF_ROWS + at + CLASS_ROWS, :] = term[0:CLASS_ROWS, F:]
+        terms[left, at : at + CLASS_ROWS, :] = term[0:CLASS_ROWS, 0:F]
+        terms[right, at : at + CLASS_ROWS, :] = term[0:CLASS_ROWS, F:]
     back[0:SEEDS, :] = jnp.dot(g, w2s[...], preferred_element_type=f32)
     back[SEEDS:, :] = jnp.dot(g, w2n[...], preferred_element_type=f32) / FAN1
 
@@ -181,11 +180,13 @@
         return carry
 
     lax.fori_loop(1, FAN1 + 1, add_block, 0)
-    terms_out[0:256, :] = w1_acc[:, 0:F]
-    terms_out[HALF_ROWS : HALF_ROWS + 256, :] = w1_acc[:, F:]
-
-
-def train(counts, where_hot, nbr1, nbr2, mid_self, hot, cold, labels, w1_self, w1_neigh, w2_self_t, w2_neigh_t):
+    terms[left, 0:256, :] = w1_acc[:, 0:F]
+    terms[right, 0:256, :] = w1_acc[:, F:]
+    keep_out[...] = terms[0]
+    send_out[...] = terms[1]
+
+
+def train(counts, where_hot, core, nbr1, nbr2, mid_self, hot, cold, labels, w1_self, w1_neigh, w2_self_t, w2_neigh_t):
     smem = pl.BlockSpec(memory_space=pltpu.SMEM)
     vmem = pl.BlockSpec(memory_space=pltpu.VMEM)
     anywhere = pl.BlockSpec(memory_space=pl.ANY)
@@ -194,14 +195,15 @@
         train_kernel,
         out_shape=(
             jax.ShapeDtypeStruct((1, SEEDS), jnp.float32),
-            jax.ShapeDtypeStruct((TERM_ROWS, F), jnp.float32),
+            jax.ShapeDtypeStruct((HALF_ROWS, F), jnp.float32),
+            jax.ShapeDtypeStruct((HALF_ROWS, F), jnp.float32),
         ),
-        in_specs=[smem] * 2 + [anywhere] * 4 + [vmem] * 10,
-        out_specs=(vmem, vmem),
+        in_specs=[smem] * 3 + [anywhere] * 4 + [vmem] * 10,
+        out_specs=(vmem, vmem, vmem),
         scratch_shapes=[
             pltpu.SMEM((SLOTS + 128,), jnp.int32),
             *[pltpu.SMEM((MID,), jnp.int32) for _ in range(FAN0 + 1)],
-            pltpu.SemaphoreType.DMA((FAN0 + FAN1 + 3,)),
+            pltpu.SemaphoreType.DMA((2 * FAN0 + FAN1 + 5,)),
             pltpu.VMEM((HOT_ROWS + COLD_ROWS, F), jnp.float32),
             pltpu.VMEM((STEP, 2 * F), jnp.float32),
             pltpu.VMEM((STEP, 2 * F), jnp.float32),
@@ -215,28 +217,73 @@
             pltpu.VMEM((SEEDS, 256), jnp.bfloat16),
             pltpu.VMEM((2 * SEEDS, HID), jnp.float32),
             pltpu.VMEM((2 * F, HID), jnp.float32),
+            pltpu.VMEM((2, HALF_ROWS, F), jnp.float32),
         ],
         compiler_params=pltpu.CompilerParams(vmem_limit_bytes=44 << 20),
         cost_estimate=pl.CostEstimate(flops=4 << 30, bytes_accessed=4 << 20, transcendentals=2 << 20),
         name="train",
     )(
-        counts, where_hot, jnp.asarray(first_slots), nbr1[:, None], nbr2[:, None], mid_self[None],
+        counts, where_hot, core, jnp.asarray(first_slots), nbr1[:, None], nbr2[:, None], mid_self[None],
         *hot, cold, labels, w1_self, w1_neigh, w2_self_t, w2_neigh_t,
     )
 
 
-def swap_hot(hot_shard, hot_ids):
+def pick_kernel(n, *refs):
+    asked, shard, given = refs[:n], refs[n], refs[n + 1 : 2 * n + 1]
+    narrow, wide, picked, copied = refs[2 * n + 1 :]
+    step = shard.shape[0] // PARTS
+    parts = [pl.ds(i * step, step) for i in range(PARTS)]
+    copies = [
+        pltpu.make_async_copy(shard.at[part], narrow.at[part], copied.at[i])
+        for i, part in enumerate(parts)
+    ]
+    for copy in copies:
+        copy.start()
+    for copy, part in zip(copies, parts):
+        copy.wait()
+        wide[part, :] = narrow[part, :].astype(jnp.float32)
+    row = 0
+    for ids, out in zip(asked, given):
+        first = row
+        for at in np.ndindex(ids.shape):
+            picked[row : row + 1, :] = wide[pl.ds(ids[at], 1), :]
+            row += 1
+        if len(out.shape) == 2:
+            out[...] = picked[first:row, :].astype(out.dtype)
+        else:
+            size = out.shape[1]
+            for o in range(out.shape[0]):
+                out[o] = picked[first + o * size : first + (o + 1) * size, :].astype(out.dtype)
+
+
+def pick_rows(shard, asked, name):
+    n = len(asked)
+    total = sum(int(np.prod(ids.shape)) for ids in asked)
+    return pl.pallas_call(
+        lambda *refs: pick_kernel(n, *refs),
+        out_shape=tuple(jax.ShapeDtypeStruct(ids.shape + (F,), jnp.bfloat16) for ids in asked),
+        in_specs=[pl.BlockSpec(memory_space=pltpu.SMEM)] * n + [pl.BlockSpec(memory_space=pltpu.HBM)],
+        out_specs=tuple(pl.BlockSpec(memory_space=pltpu.VMEM) for _ in asked),
+        scratch_shapes=[
+            pltpu.VMEM(shard.shape, shard.dtype),
+            pltpu.VMEM(shard.shape, jnp.float32),
+            pltpu.VMEM((total, F), jnp.float32),
+            pltpu.SemaphoreType.DMA((PARTS,)),
+        ],
+        compiler_params=pltpu.CompilerParams(vmem_limit_bytes=40 << 20),
+        cost_estimate=pl.CostEstimate(flops=0, bytes_accessed=4 << 20, transcendentals=0),
+        name=name,
+    )(*asked, shard)
+
+
+def clique_peers(hot_ids):
     me = lax.axis_index("clique")
     peers = [lax.rem(me + d, 4) for d in range(4)]
-    asked = [lax.dynamic_index_in_dim(hot_ids, peer, 0, keepdims=False) for peer in peers]
-    requests = [asked[0]] + [
-        lax.ppermute(asked[d], "clique", [(i, (i + d) % 4) for i in range(4)]) for d in (1, 2, 3)
-    ]
-    return peers, requests
-
-
-def serve_hot(hot_shard, requests):
-    rows = [hot_shard.at[ids].get(mode="promise_in_bounds") for ids in requests]
+    return peers, [lax.dynamic_index_in_dim(hot_ids, peer, 0, keepdims=False) for peer in peers]
+
+
+def fetch_hot(hot_shard, requests):
+    rows = pick_rows(hot_shard, requests, "pick_hot")
     return [rows[0]] + [
         lax.ppermute(rows[d], "clique", [(i, (i - d) % 4) for i in range(4)]) for d in (1, 2, 3)
     ]
@@ -253,45 +300,51 @@
 SWAP = [(0, 1), (1, 0)]
 
 
-def sum_everywhere(x):
-    tiles = x.reshape(TERM_ROWS // 8, 8, F)
-    half = tiles.shape[0] // 2
-    core = lax.axis_index("core")
-    theirs = lax.dynamic_slice_in_dim(tiles, (1 - core) * half, half, 0)
-    mine = lax.dynamic_slice_in_dim(tiles, core * half, half, 0)
-    mine = mine + lax.ppermute(theirs, "core", SWAP)
-    mine = exchange(mine.reshape(16, half // 16, 8, F), ("clique", "y")).sum(0)
+def split_kernel(core, mine, other, *outs):
+    for first, at in ((0, slice(0, F)), (1, slice(F, 2 * F))):
+        for out, row in zip(outs, (0, F, 2 * F, 2 * F + CLASS_ROWS)):
+            rows = slice(row, row + out.shape[0])
+            out[:, at] = jnp.where(core[0] == first, mine[rows, :], other[rows, :])
+
+
+def sum_everywhere(keep, send, core):
+    mine = keep + lax.ppermute(send, "core", SWAP)
+    mine = exchange(mine.reshape(16, HALF_ROWS // 128, 8, F), ("clique", "y")).sum(0)
     mine = share(mine, "z", 8).sum(0)
-    mine = share(mine, ("clique", "y"), 16).reshape(half * 8, F)
+    mine = share(mine, ("clique", "y"), 16).reshape(HALF_ROWS, F)
     other = lax.ppermute(mine, "core", SWAP)
-    return jnp.where(core == 0, mine, other), jnp.where(core == 0, other, mine)
+    vmem = pl.BlockSpec(memory_space=pltpu.VMEM)
+    return pl.pallas_call(
+        split_kernel,
+        out_shape=tuple(jax.ShapeDtypeStruct((n, HID), jnp.float32) for n in (F, F, CLASSES, CLASSES)),
+        in_specs=[pl.BlockSpec(memory_space=pltpu.SMEM), vmem, vmem],
+        out_specs=(vmem,) * 4,
+        compiler_params=pltpu.CompilerParams(vmem_limit_bytes=8 << 20),
+        name="split",
+    )(core, mine, other)
 
 
 def body(
     hot_shard, cold_shard, hot_ids, cold_ids, cold_counts, mid_self, nbr1, nbr2, labels,
     w1_self, w1_neigh, w2_self, w2_neigh,
 ):
-    peers, requests = swap_hot(hot_shard, hot_ids[0])
-    asked = exchange(cold_ids[0], GROUP)
-    served = cold_shard.at[asked].get(mode="promise_in_bounds")
+    peers, hot_asked = clique_peers(hot_ids[0])
+    hot_asked[1:] = [
+        lax.ppermute(hot_asked[d], "clique", [(i, (i + d) % 4) for i in range(4)]) for d in (1, 2, 3)
+    ]
+    cold_asked = exchange(cold_ids[0], GROUP)
+    *hot_asked, cold_asked = lax.optimization_barrier((*hot_asked, cold_asked))
+    (served,) = pick_rows(cold_shard, [cold_asked], "pick_cold")
     cold = exchange(served, GROUP)
-    hot = serve_hot(hot_shard, requests)
-    loss, terms = train(
-        cold_counts[0], jnp.stack(peers).astype(jnp.int32), nbr1[0], nbr2[0], mid_self[0],
+    *hot_asked, served = lax.optimization_barrier((*hot_asked, served))
+    hot = fetch_hot(hot_shard, hot_asked)
+    core = lax.axis_index("core").astype(jnp.int32)[None]
+    loss, keep, send = train(
+        cold_counts[0], jnp.stack(peers).astype(jnp.int32), core, nbr1[0], nbr2[0], mid_self[0],
         hot, cold, labels, w1_self, w1_neigh, w2_self.T, w2_neigh.T,
     )
-    left, right = sum_everywhere(terms)
-
-    def rows(at, n):
-        return jnp.concatenate([left[at : at + n], right[at : at + n]], axis=1)
-
-    return (
-        loss,
-        rows(0, F),
-        rows(F, F),
-        rows(2 * F, CLASSES).T,
-        rows(2 * F + CLASS_ROWS, CLASSES).T,
-    )
+    w1s, w1n, w2s, w2n = sum_everywhere(keep, send, core)
+    return loss, w1s, w1n, w2s.T, w2n.T
 
 
 def solution(mesh):

time: 189 us -> 178 us (0.942)
  local copies, waits for them, and re-layouts: 28.1 us -> 6.74 us
  waiting for transfers between devices: 6.7 us -> 16.8 us
  Pallas kernels: 75.4 us -> 80.8 us
  other arithmetic: 3.66 us -> 0.15 us
  blocking collectives: 39.7 us -> 36.8 us
    gather x5 -> x0, local copies, waits for them, and re-layouts: 25.6 us -> none  [the longest x4 15.1 us: serve_hot(): rows = [hot_shard.at[ids].get(mode='promise_in_bounds') for ids in requests]]
    ppermute x7, waiting for transfers between devices: 1.27 us -> 12.5 us  [the longest x3 8.54 us: fetch_hot(): lax.ppermute(rows[d], 'clique', [(i, (i - d) % 4) for i in range(4)])]
    pallas_call x0 -> x3, Pallas kernels: none -> 7.55 us  [the longest x2 6.69 us: pick_rows(): pl.pallas_call(lambda *refs: pick_kernel(n, *refs), out_shape=tuple((jax....]
    unnamed x21 -> x25, local copies, waits for them, and re-layouts: 1.48 us -> 5.84 us
    all_to_all x2, starting transfers between devices: 20.1 us -> 23.5 us  [exchange(): return lax.all_to_all(x, axes, split_axis=0, concat_axis=0, tiled=True)]
    all_to_all x3, blocking collectives: 39.7 us -> 36.8 us  [exchange(): return lax.all_to_all(x, axes, split_axis=0, concat_axis=0, tiled=True)]
    ppermute x7, starting transfers between devices: 9.54 us -> 7.24 us  [the longest x3 4.29 us: body(): lax.ppermute(hot_asked[d], 'clique', [(i, (i + d) % 4) for i in range(4)])]
    pallas_call x1, Pallas kernels: 75.4 us -> 73.2 us  [train(): pl.pallas_call(train_kernel, out_shape=(jax.ShapeDtypeStruct((1, SEEDS),...]
  transfers between devices with their start and end apart: 10 -> 10, of which waited for: 3 -> 8; matrix products, arithmetic and copies ran while one was open for 15% -> 1% of each run, Pallas kernels for 0% -> 2%
where the time goes in v2:
time: 178 us; the launch traced here: 177 us
  Pallas kernels  80.8 us (45%)
  blocking collectives  36.8 us (21%)
  starting transfers between devices  35 us (20%)
  waiting for transfers between devices  16.8 us (9%)
  local copies, waits for them, and re-layouts  6.74 us (4%)
    pallas_call x1, Pallas kernels, train(): pl.pallas_call(train_kernel, out_shape=(jax.ShapeDtypeStruct((1, SEEDS),...  73.2 us
    all_to_all x3, blocking collectives, exchange(): return lax.all_to_all(x, axes, split_axis=0, concat_axis=0, tiled=True)  36.8 us
    all_to_all x2, starting transfers between devices, exchange(): return lax.all_to_all(x, axes, split_axis=0, concat_axis=0, tiled=True)  23.5 us
    ppermute x3, waiting for transfers between devices, fetch_hot(): lax.ppermute(rows[d], 'clique', [(i, (i - d) % 4) for i in range(4)])  8.54 us
    pallas_call x2, Pallas kernels, pick_rows(): pl.pallas_call(lambda *refs: pick_kernel(n, *refs), out_shape=tuple((jax....  6.69 us
    unnamed x25, local copies, waits for them, and re-layouts  5.84 us
    ppermute x1, starting transfers between devices, sum_everywhere(): other = lax.ppermute(mine, 'core', SWAP)  4.32 us
    ppermute x3, starting transfers between devices, body(): lax.ppermute(hot_asked[d], 'clique', [(i, (i + d) % 4) for i in range(4)])  4.29 us
  transfers between devices with their start and end apart: 10, of which 8 were waited for; matrix products, arithmetic and copies ran while one was open for 1% of the time, Pallas kernels for 2%

profile of v2, /device:TPU:1, one launch (start us, length us, event | category | flops | bytes accessed | tf_op | source)
XLA Modules:
  0.0 177.2 jit_solution(637836962594085016)
XLA Ops:
  0.6 1.4 copy.21
  2.0 13.2 %all-to-all-start = ((s32[64,1,32]{2,1,0:T(1,128)}), s32[64,1,32]{2,1,0:T(1,128)S(1)}, u32[]{:S(2)}, u32[]{:S(2)}) async-start(s32[64,1,32]{2,1,0:T(1,128)} %bitcast.12), calls=%async_computation | async-start | bytes 65536 | tf_op jit(solution)/shard_map/all_to_all | solution.py:293
  15.2 0.9 constant_dynamic-slice_fusion
  16.1 1.3 collective-permute-start
  17.4 1.5 collective-permute-start.2
  18.9 1.5 collective-permute-start.1
  20.4 2.7 %collective-permute-done.1.refs_2_ = s32[512]{0:T(512)S(1)} collective-permute-done((s32[512]{0:T(512)S(1)}, s32[512]{0:T(512)S(1)}, u32[]{:S(2)}, u32[]{:S(2)}) %collective-permute-start.1) | collective-permute-done | bytes 2080 | tf_op jit(solution)/shard_map/ppermute | solution.py:333
  23.1 1.4 all-to-all-done
  24.5 2.2 %copy-done = bf16[16384,128]{1,0:T(8,128)(2,1)S(1)} copy-done((bf16[16384,128]{1,0:T(8,128)(2,1)S(1)}, bf16[16384,128]{1,0:T(8,128)(2,1)}, u32[]{:S(2)}) %copy-start) | copy-done | bytes 4194328
  26.7 0.0 copy-start.6
  26.8 0.0 copy-start.11
  26.8 3.9 %pick_cold.1 = bf16[64,32,128]{2,1,0:T(8,128)(2,1)} custom-call(s32[64,32]{1,0:T(8,128)S(1)} %bitcast.22, bf16[16384,128]{1,0:T(8,128)(2,1)S(1)} %copy-done), custom_call_target="tpu_custom_call" | custom-call | bytes 4194304 | tf_op jit(solution)/shard_map/pick_cold/pallas_call | solution.py:262
  30.7 10.3 %all-to-all-start.1 = ((bf16[64,32,128]{2,1,0:T(8,128)(2,1)}), bf16[64,32,128]{2,1,0:T(8,128)(2,1)S(1)}, u32[]{:S(2)}, u32[]{:S(2)}) async-start(bf16[64,32,128]{2,1,0:T(8,128)(2,1)} %pick_cold.1), calls=%async_computation.1 | async-start | bytes 1048576 | tf_op jit(solution)/shard_map/all_to_all | solution.py:293
  41.0 2.2 %copy-done.1 = bf16[16384,128]{1,0:T(8,128)(2,1)S(1)} copy-done((bf16[16384,128]{1,0:T(8,128)(2,1)S(1)}, bf16[16384,128]{1,0:T(8,128)(2,1)}, u32[]{:S(2)}) %copy-start.1) | copy-done | bytes 4194328
  43.2 2.8 %pick_hot.1 = (bf16[512,128]{1,0:T(8,128)(2,1)S(1)}, bf16[512,128]{1,0:T(8,128)(2,1)S(1)}, bf16[512,128]{1,0:T(8,128)(2,1)S(1)}, bf16[512,128]{1,0:T(8,128)(2,1)S(1)}) custom-call(s32[512]{0:T(512)S(1)} %bitcast.23, s32[512]{0:T(512)S(1)} %collective-permute-done.refs_1_, s32[512]{0:T(512)S(1)} %collective-permute-done.1.refs_2_, ...), custom_call_target="tpu_custom_call" | custom-call | bytes 4194304 | tf_op jit(solution)/shard_map/pick_hot/pallas_call | solution.py:262
  46.0 1.4 collective-permute-start.3
  47.4 0.5 collective-permute-start.4
  47.9 0.6 collective-permute-start.5
  48.5 0.1 pad_add_fusion.where_hot
  48.6 2.1 %collective-permute-done.3.hot1 = bf16[512,128]{1,0:T(8,128)(2,1)S(1)} collective-permute-done((bf16[512,128]{1,0:T(8,128)(2,1)S(1)}, bf16[512,128]{1,0:T(8,128)(2,1)S(1)}, u32[]{:S(2)}, u32[]{:S(2)}) %collective-permute-start.3) | collective-permute-done | bytes 131104 | tf_op jit(solution)/shard_map/ppermute | solution.py:288
  50.7 2.5 %collective-permute-done.4.hot2 = bf16[512,128]{1,0:T(8,128)(2,1)S(1)} collective-permute-done((bf16[512,128]{1,0:T(8,128)(2,1)S(1)}, bf16[512,128]{1,0:T(8,128)(2,1)S(1)}, u32[]{:S(2)}, u32[]{:S(2)}) %collective-permute-start.4) | collective-permute-done | bytes 131104 | tf_op jit(solution)/shard_map/ppermute | solution.py:288
  53.2 3.9 %collective-permute-done.5.hot3 = bf16[512,128]{1,0:T(8,128)(2,1)S(1)} collective-permute-done((bf16[512,128]{1,0:T(8,128)(2,1)S(1)}, bf16[512,128]{1,0:T(8,128)(2,1)S(1)}, u32[]{:S(2)}, u32[]{:S(2)}) %collective-permute-start.5) | collective-permute-done | bytes 131104 | tf_op jit(solution)/shard_map/ppermute | solution.py:288
  57.1 1.7 all-to-all-done.1.cold
  58.8 73.2 %train.1 = (f32[1,512]{1,0:T(1,128)}, f32[640,128]{1,0:T(8,128)S(1)}, f32[640,128]{1,0:T(8,128)S(1)}) custom-call(s32[64]{0:T(128)S(1)} %bitcast.28, s32[4]{0:T(128)S(1)} %pad_add_fusion.where_hot, s32[1]{0:T(128)} %bitcast.5.core, s32[1,512]{1,0:T(1,128)S(1)} %copy-done.11, s32[10,1,7680]{2,1,0:T(1,128)S(1)} %bitcast.24, s32[15,1,512]{2,1,0:T(1,128)S(1)} %bitcast.27, ...), custom_call_target="tpu_custom_call" | custom-call | flops 4294967296 | bytes 4194304 | tf_op jit(solution)/shard_map/train/pallas_call | solution.py:194
  132.1 0.5 collective-permute-start.6
  132.6 1.3 collective-permute-done.6
  133.9 13.1 %all_to_all.32 = f32[16,5,8,128]{3,2,1,0:T(8,128)S(1)} all-to-all(f32[16,5,8,128]{3,2,1,0:T(8,128)S(1)} %bitcast.29), channel_id=1, replica_groups=mesh['clique'=4,'z'=8,'y'=4,'core'=2] {'clique','y'}, dimensions={0} | all-to-all | bytes 655360 | tf_op jit(solution)/shard_map/all_to_all | solution.py:293
  147.0 12.3 %all_to_all.33 = f32[8,5,8,128]{3,2,1,0:T(8,128)S(1)} all-to-all(f32[8,5,8,128]{3,2,1,0:T(8,128)S(1)} %broadcast_in_dim.7), channel_id=1, replica_groups=mesh['clique'=4,'z'=8,'y'=4,'core'=2] {'z'}, dimensions={0} | all-to-all | bytes 327680 | tf_op jit(solution)/shard_map/all_to_all | solution.py:293
  159.3 11.5 %all_to_all.34 = f32[16,5,8,128]{3,2,1,0:T(8,128)S(1)} all-to-all(f32[16,5,8,128]{3,2,1,0:T(8,128)S(1)} %broadcast_in_dim.8), channel_id=1, replica_groups=mesh['clique'=4,'z'=8,'y'=4,'core'=2] {'clique','y'}, dimensions={0} | all-to-all | bytes 655360 | tf_op jit(solution)/shard_map/all_to_all | solution.py:293
  170.8 4.3 %collective-permute-start.7 = (f32[640,128]{1,0:T(8,128)S(1)}, f32[640,128]{1,0:T(8,128)S(1)}, u32[]{:S(2)}, u32[]{:S(2)}) collective-permute-start(f32[640,128]{1,0:T(8,128)S(1)} %bitcast.20), channel_id=1, source_target_pairs={{0,1},{1,0},{2,3},{3,2},{4,5},{5,4},{6,7},{7,6},{8,9},{9,8},{10,11... | collective-permute-start | bytes 983048 | tf_op jit(solution)/shard_map/ppermute | solution.py:315
  175.1 1.3 collective-permute-done.7.other
  176.4 0.9 split.1
  (27 shorter events, 0.2 us)
Async XLA Ops:
  2.0 22.5 %all-to-all-start = ((s32[64,1,32]{2,1,0:T(1,128)}), s32[64,1,32]{2,1,0:T(1,128)S(1)}, u32[]{:S(2)}, u32[]{:S(2)}) async-start(s32[64,1,32]{2,1,0:T(1,128)} %bitcast.12), calls=%async_computation | async-start | bytes 65536 | tf_op jit(solution)/shard_map/all_to_all | solution.py:293
  16.1 4.3 %collective-permute-start = (s32[512]{0:T(512)S(1)}, s32[512]{0:T(512)S(1)}, u32[]{:S(2)}, u32[]{:S(2)}) collective-permute-start(s32[512]{0:T(512)S(1)} %bitcast.32), channel_id=1, source_target_pairs={{0,64},{64,128},{128,192},{192,0},{1,65},{65,129},{129,193},{193,1... | collective-permute-start | bytes 6152 | tf_op jit(solution)/shard_map/ppermute | solution.py:333
  17.4 3.0 %collective-permute-start.2 = (s32[512]{0:T(512)S(1)}, s32[512]{0:T(512)S(1)}, u32[]{:S(2)}, u32[]{:S(2)}) collective-permute-start(s32[512]{0:T(512)S(1)} %bitcast.31), channel_id=1, source_target_pairs={{0,192},{64,0},{128,64},{192,128},{1,193},{65,1},{129,65},{193,129... | collective-permute-start | bytes 6152 | tf_op jit(solution)/shard_map/ppermute | solution.py:333
  18.9 4.2 %collective-permute-start.1 = (s32[512]{0:T(512)S(1)}, s32[512]{0:T(512)S(1)}, u32[]{:S(2)}, u32[]{:S(2)}) collective-permute-start(s32[512]{0:T(512)S(1)} %bitcast.30), channel_id=1, source_target_pairs={{0,128},{64,192},{128,0},{192,64},{1,129},{65,193},{129,1},{193,65... | collective-permute-start | bytes 6152 | tf_op jit(solution)/shard_map/ppermute | solution.py:333
  24.5 2.2 %copy-start = (bf16[16384,128]{1,0:T(8,128)(2,1)S(1)}, bf16[16384,128]{1,0:T(8,128)(2,1)}, u32[]{:S(2)}) copy-start(bf16[16384,128]{1,0:T(8,128)(2,1)} %refs_1_.1) | copy-start | bytes 12582916
  26.7 32.1 %copy-start.2 = (s32[1,10,7680]{2,0,1:T(1,128)S(1)}, s32[1,10,7680]{2,0,1:T(1,128)}, u32[]{:S(2)}) copy-start(s32[1,10,7680]{2,0,1:T(1,128)} %param.20) | copy-start | bytes 921604
  26.7 32.1 %copy-start.3 = (bf16[256,172]{0,1:T(8,128)(2,1)S(1)}, bf16[256,172]{0,1:T(8,128)(2,1)}, u32[]{:S(2)}) copy-start(bf16[256,172]{0,1:T(8,128)(2,1)} %param.25) | copy-start | bytes 264196
  26.7 32.1 %copy-start.4 = (bf16[256,172]{0,1:T(8,128)(2,1)S(1)}, bf16[256,172]{0,1:T(8,128)(2,1)}, u32[]{:S(2)}) copy-start(bf16[256,172]{0,1:T(8,128)(2,1)} %param.26) | copy-start | bytes 264196
  26.7 32.1 %copy-start.5 = (bf16[128,256]{1,0:T(8,128)(2,1)S(1)}, bf16[128,256]{1,0:T(8,128)(2,1)}, u32[]{:S(2)}) copy-start(bf16[128,256]{1,0:T(8,128)(2,1)} %w1_self.1) | copy-start | bytes 196612
  26.7 32.1 %copy-start.6 = (bf16[128,256]{1,0:T(8,128)(2,1)S(1)}, bf16[128,256]{1,0:T(8,128)(2,1)}, u32[]{:S(2)}) copy-start(bf16[128,256]{1,0:T(8,128)(2,1)} %w1_neigh.1) | copy-start | bytes 196612
  26.7 32.1 %copy-start.7 = (s32[1,15,512]{2,0,1:T(1,128)S(1)}, s32[1,15,512]{2,0,1:T(1,128)}, u32[]{:S(2)}) copy-start(s32[1,15,512]{2,0,1:T(1,128)} %param.21) | copy-start | bytes 92164
  26.7 32.1 %copy-start.8 = (s32[1,7680]{1,0:T(1,128)S(1)}, s32[1,7680]{1,0:T(1,128)}, u32[]{:S(2)}) copy-start(s32[1,7680]{1,0:T(1,128)} %mid_self.1) | copy-start | bytes 92164
  26.7 32.1 %copy-start.9 = (s32[1,512]{1,0:T(1,128)S(1)}, s32[1,512]{1,0:T(1,128)}, u32[]{:S(2)}) copy-start(s32[1,512]{1,0:T(1,128)} %labels.1) | copy-start | bytes 6148
  26.8 32.1 %copy-start.10 = (s32[1,64]{1,0:T(1,128)S(1)}, s32[1,64]{1,0:T(1,128)}, u32[]{:S(2)}) copy-start(s32[1,64]{1,0:T(1,128)} %param.18) | copy-start | bytes 772
  26.8 32.1 %copy-start.11 = (s32[1,512]{1,0:T(1,128)S(1)}, s32[1,512]{1,0:T(1,128)}, u32[]{:S(2)}) copy-start(s32[1,512]{1,0:T(1,128)} %constant.45.clone.first_slots) | copy-start | bytes 6148
  30.7 28.0 %all-to-all-start.1 = ((bf16[64,32,128]{2,1,0:T(8,128)(2,1)}), bf16[64,32,128]{2,1,0:T(8,128)(2,1)S(1)}, u32[]{:S(2)}, u32[]{:S(2)}) async-start(bf16[64,32,128]{2,1,0:T(8,128)(2,1)} %pick_cold.1), calls=%async_computation.1 | async-start | bytes 1048576 | tf_op jit(solution)/shard_map/all_to_all | solution.py:293
  41.0 2.2 %copy-start.1 = (bf16[16384,128]{1,0:T(8,128)(2,1)S(1)}, bf16[16384,128]{1,0:T(8,128)(2,1)}, u32[]{:S(2)}) copy-start(bf16[16384,128]{1,0:T(8,128)(2,1)} %refs_4_.1) | copy-start | bytes 12582916
  46.0 4.7 %collective-permute-start.3 = (bf16[512,128]{1,0:T(8,128)(2,1)S(1)}, bf16[512,128]{1,0:T(8,128)(2,1)S(1)}, u32[]{:S(2)}, u32[]{:S(2)}) collective-permute-start(bf16[512,128]{1,0:T(8,128)(2,1)S(1)} %get-tuple-element.35), channel_id=1, source_target_pairs={{0,192},{64,0},{128,64},{192,128},{1,193},{65,1},{129,65},{193,129... | collective-permute-start | bytes 393224 | tf_op jit(solution)/shard_map/ppermute | solution.py:288
  47.4 5.8 %collective-permute-start.4 = (bf16[512,128]{1,0:T(8,128)(2,1)S(1)}, bf16[512,128]{1,0:T(8,128)(2,1)S(1)}, u32[]{:S(2)}, u32[]{:S(2)}) collective-permute-start(bf16[512,128]{1,0:T(8,128)(2,1)S(1)} %get-tuple-element.36), channel_id=1, source_target_pairs={{0,128},{64,192},{128,0},{192,64},{1,129},{65,193},{129,1},{193,65... | collective-permute-start | bytes 393224 | tf_op jit(solution)/shard_map/ppermute | solution.py:288
  47.9 9.2 %collective-permute-start.5 = (bf16[512,128]{1,0:T(8,128)(2,1)S(1)}, bf16[512,128]{1,0:T(8,128)(2,1)S(1)}, u32[]{:S(2)}, u32[]{:S(2)}) collective-permute-start(bf16[512,128]{1,0:T(8,128)(2,1)S(1)} %get-tuple-element.37), channel_id=1, source_target_pairs={{0,64},{64,128},{128,192},{192,0},{1,65},{65,129},{129,193},{193,1... | collective-permute-start | bytes 393224 | tf_op jit(solution)/shard_map/ppermute | solution.py:288
  132.1 1.7 collective-permute-start.6
  170.8 5.6 %collective-permute-start.7 = (f32[640,128]{1,0:T(8,128)S(1)}, f32[640,128]{1,0:T(8,128)S(1)}, u32[]{:S(2)}, u32[]{:S(2)}) collective-permute-start(f32[640,128]{1,0:T(8,128)S(1)} %bitcast.20), channel_id=1, source_target_pairs={{0,1},{1,0},{2,3},{3,2},{4,5},{5,4},{6,7},{7,6},{8,9},{9,8},{10,11... | collective-permute-start | bytes 983048 | tf_op jit(solution)/shard_map/ppermute | solution.py:315

commit v3 on v2

--- a/solution.py
+++ b/solution.py
@@ -16,6 +16,7 @@
 SEEDS = 512
 MID = 7680
 FAN0 = 10
+POSITIONS = FAN0 + 1
 FAN1 = 15
 HOT_ROWS = 2048
 COLD_ROWS = 2048
@@ -25,6 +26,7 @@
 SEED_CHUNKS = SEEDS // STEP
 HALF_ROWS = 640
 PARTS = 8
+PIECES = (0, 512, 2048, SLOTS)
 GELU_C = float(np.sqrt(2.0 / np.pi))
 GELU_A = 0.044715
 
@@ -38,30 +40,86 @@
     return rows[0]
 
 
+def order_kernel(nbr2, nbr1, mid_self, out, slots, info, ordered, copied):
+    copies = [
+        pltpu.make_async_copy(nbr2.at[k, 0], slots.at[pl.ds(k * SEEDS, SEEDS)], copied.at[k])
+        for k in range(FAN1)
+    ]
+    for copy in copies:
+        copy.start()
+    empty = jnp.zeros((128 - POSITIONS, 128), jnp.int32)
+
+    def by_node(i, carry):
+        at = pl.ds(pl.multiple_of(i * 128, 128), 128)
+        rows = [nbr1[k, :, at] for k in range(FAN0)] + [mid_self[:, at]]
+        info[at, :] = jnp.concatenate([*rows, empty], axis=0).T
+        return carry
+
+    lax.fori_loop(0, MID // 128, by_node, 0, unroll=4)
+    for k in range(FAN0):
+        out[k, :, 0:SEEDS] = nbr1[k, :, 0:SEEDS]
+    out[FAN0, :, 0:SEEDS] = mid_self[:, 0:SEEDS]
+    for copy in copies:
+        copy.wait()
+
+    def by_slot(i, carry):
+        base = i * 128
+        for u in range(128):
+            ordered[pl.ds(base + u, 1), :] = info[pl.ds(slots[base + u], 1), :]
+        return carry
+
+    lax.fori_loop(0, MID // 128, by_slot, 0)
+
+    def by_chunk(i, carry):
+        rows = ordered[pl.ds(pl.multiple_of(i * 128, 128), 128), :].T
+        at = pl.ds(pl.multiple_of(SEEDS + i * 128, 128), 128)
+        for k in range(POSITIONS):
+            out[k, :, at] = rows[k : k + 1, :]
+        return carry
+
+    lax.fori_loop(0, MID // 128, by_chunk, 0, unroll=4)
+
+
+def order_positions(nbr1, nbr2, mid_self):
+    vmem = pl.BlockSpec(memory_space=pltpu.VMEM)
+    return pl.pallas_call(
+        order_kernel,
+        out_shape=jax.ShapeDtypeStruct((POSITIONS, 1, SLOTS), jnp.int32),
+        in_specs=[pl.BlockSpec(memory_space=pl.ANY), vmem, vmem],
+        out_specs=vmem,
+        scratch_shapes=[
+            pltpu.SMEM((MID,), jnp.int32),
+            pltpu.VMEM((MID, 128), jnp.int32),
+            pltpu.VMEM((MID, 128), jnp.int32),
+            pltpu.SemaphoreType.DMA((FAN1,)),
+        ],
+        compiler_params=pltpu.CompilerParams(vmem_limit_bytes=16 << 20),
+        cost_estimate=pl.CostEstimate(flops=0, bytes_accessed=8 << 20, transcendentals=0),
+        name="order",
+    )(nbr2[:, None], nbr1[:, None], mid_self[None])
+
+
 def train_kernel(
-    counts, where_hot, core, first_slots, nbr1, nbr2, mid_self,
+    counts, where_hot, core, places,
     hot0, hot1, hot2, hot3, cold, labels, w1_self, w1_neigh, w2_self, w2_neigh,
     loss_out, keep_out, send_out,
-    slots, n0, n1, n2, n3, n4, n5, n6, n7, n8, n9, own, copied,
+    n0, n1, n2, n3, n4, n5, n6, n7, n8, n9, own, copied,
     table, x_even, x_odd, w1, w2s, w2n, x_all, slope, hidden, hidden_b, grad_logits, back, w1_acc, terms,
 ):
     f32, bf16 = jnp.float32, jnp.bfloat16
     neighbours = (n0, n1, n2, n3, n4, n5, n6, n7, n8, n9)
-    head, tail = pl.ds(0, SEEDS), pl.ds(SEEDS, MID - SEEDS)
-    early, late = [], []
-    for k in range(FAN0):
-        early.append((nbr1.at[k, 0, head], neighbours[k].at[head]))
-        late.append((nbr1.at[k, 0, tail], neighbours[k].at[tail]))
-    early.append((mid_self.at[0, head], own.at[head]))
-    late.append((mid_self.at[0, tail], own.at[tail]))
-    early.append((first_slots.at[0], slots.at[head]))
-    late.append((first_slots.at[0, pl.ds(0, STEP)], slots.at[pl.ds(SLOTS, STEP)]))
-    for k in range(FAN1):
-        late.append((nbr2.at[k, 0], slots.at[pl.ds((k + 1) * SEEDS, SEEDS)]))
-    early = [pltpu.make_async_copy(*pair, copied.at[i]) for i, pair in enumerate(early)]
-    late = [pltpu.make_async_copy(*pair, copied.at[len(early) + i]) for i, pair in enumerate(late)]
-    for copy in early + late:
-        copy.start()
+    pieces = []
+    for p, (start, stop) in enumerate(zip(PIECES[:-1], PIECES[1:])):
+        at = pl.ds(start, stop - start)
+        pieces.append(
+            [
+                pltpu.make_async_copy(places.at[k, 0, at], to.at[at], copied.at[p, k])
+                for k, to in enumerate((*neighbours, own))
+            ]
+        )
+    for copies in pieces:
+        for copy in copies:
+            copy.start()
 
     for d, block in enumerate((hot0, hot1, hot2, hot3)):
         start = pl.multiple_of(where_hot[d] * 512, 512)
@@ -86,7 +144,7 @@
     def gather(chunk, buffer):
         base = chunk * STEP
         for u in range(STEP):
-            m = slots[base + u]
+            m = base + u
             rows = [table[pl.ds(near[m], 1), :] for near in neighbours]
             buffer[u : u + 1, 0:F] = table[pl.ds(own[m], 1), :]
             buffer[u : u + 1, F : 2 * F] = tree_sum(rows)
@@ -111,19 +169,21 @@
         )
         hidden[pl.ds(into, STEP), :] += h
 
-    for copy in early:
+    for copy in pieces[0]:
         copy.wait()
     gather(0, x_even)
 
     def two_chunks(i, carry):
-        @pl.when(i == SEED_CHUNKS // 2 - 1)
-        def _():
-            for copy in late:
-                copy.wait()
-
         gather(2 * i + 1, x_odd)
         forward(2 * i, x_even)
-        gather(2 * i + 2, x_even)
+        for p, start in enumerate(PIECES[1:-1]):
+
+            @pl.when(2 * i + 2 == start // STEP)
+            def _():
+                for copy in pieces[p + 1]:
+                    copy.wait()
+
+        gather(lax.rem(2 * i + 2, CHUNKS), x_even)
         forward(2 * i + 1, x_odd)
         return carry
 
@@ -176,21 +236,21 @@
     w1_acc[...] = backward(0, slice(0, SEEDS))
 
     def add_block(j, carry):
-        w1_acc[...] += backward(j, slice(SEEDS, 2 * SEEDS))
-        return carry
-
-    lax.fori_loop(1, FAN1 + 1, add_block, 0)
+        terms_of = [backward(5 * j + 1 + i, slice(SEEDS, 2 * SEEDS)) for i in range(5)]
+        w1_acc[...] += tree_sum(terms_of)
+        return carry
+
+    lax.fori_loop(0, FAN1 // 5, add_block, 0)
     terms[left, 0:256, :] = w1_acc[:, 0:F]
     terms[right, 0:256, :] = w1_acc[:, F:]
     keep_out[...] = terms[0]
     send_out[...] = terms[1]
 
 
-def train(counts, where_hot, core, nbr1, nbr2, mid_self, hot, cold, labels, w1_self, w1_neigh, w2_self_t, w2_neigh_t):
+def train(counts, where_hot, core, places, hot, cold, labels, w1_self, w1_neigh, w2_self_t, w2_neigh_t):
     smem = pl.BlockSpec(memory_space=pltpu.SMEM)
     vmem = pl.BlockSpec(memory_space=pltpu.VMEM)
     anywhere = pl.BlockSpec(memory_space=pl.ANY)
-    first_slots = np.arange(SEEDS, dtype=np.int32)[None]
     return pl.pallas_call(
         train_kernel,
         out_shape=(
@@ -198,12 +258,11 @@
             jax.ShapeDtypeStruct((HALF_ROWS, F), jnp.float32),
             jax.ShapeDtypeStruct((HALF_ROWS, F), jnp.float32),
         ),
-        in_specs=[smem] * 3 + [anywhere] * 4 + [vmem] * 10,
+        in_specs=[smem] * 3 + [anywhere] + [vmem] * 10,
         out_specs=(vmem, vmem, vmem),
         scratch_shapes=[
-            pltpu.SMEM((SLOTS + 128,), jnp.int32),
-            *[pltpu.SMEM((MID,), jnp.int32) for _ in range(FAN0 + 1)],
-            pltpu.SemaphoreType.DMA((2 * FAN0 + FAN1 + 5,)),
+            *[pltpu.SMEM((SLOTS,), jnp.int32) for _ in range(POSITIONS)],
+            pltpu.SemaphoreType.DMA((len(PIECES) - 1, POSITIONS)),
             pltpu.VMEM((HOT_ROWS + COLD_ROWS, F), jnp.float32),
             pltpu.VMEM((STEP, 2 * F), jnp.float32),
             pltpu.VMEM((STEP, 2 * F), jnp.float32),
@@ -223,8 +282,7 @@
         cost_estimate=pl.CostEstimate(flops=4 << 30, bytes_accessed=4 << 20, transcendentals=2 << 20),
         name="train",
     )(
-        counts, where_hot, core, jnp.asarray(first_slots), nbr1[:, None], nbr2[:, None], mid_self[None],
-        *hot, cold, labels, w1_self, w1_neigh, w2_self_t, w2_neigh_t,
+        counts, where_hot, core, places, *hot, cold, labels, w1_self, w1_neigh, w2_self_t, w2_neigh_t,
     )
 
 
@@ -282,8 +340,7 @@
     return peers, [lax.dynamic_index_in_dim(hot_ids, peer, 0, keepdims=False) for peer in peers]
 
 
-def fetch_hot(hot_shard, requests):
-    rows = pick_rows(hot_shard, requests, "pick_hot")
+def send_hot(rows):
     return [rows[0]] + [
         lax.ppermute(rows[d], "clique", [(i, (i - d) % 4) for i in range(4)]) for d in (1, 2, 3)
     ]
@@ -337,10 +394,13 @@
     (served,) = pick_rows(cold_shard, [cold_asked], "pick_cold")
     cold = exchange(served, GROUP)
     *hot_asked, served = lax.optimization_barrier((*hot_asked, served))
-    hot = fetch_hot(hot_shard, hot_asked)
+    rows = pick_rows(hot_shard, hot_asked, "pick_hot")
+    *rows, nbr2 = lax.optimization_barrier((*rows, nbr2))
+    hot = send_hot(rows)
+    places = order_positions(nbr1[0], nbr2[0], mid_self[0])
     core = lax.axis_index("core").astype(jnp.int32)[None]
     loss, keep, send = train(
-        cold_counts[0], jnp.stack(peers).astype(jnp.int32), core, nbr1[0], nbr2[0], mid_self[0],
+        cold_counts[0], jnp.stack(peers).astype(jnp.int32), core, places,
         hot, cold, labels, w1_self, w1_neigh, w2_self.T, w2_neigh.T,
     )
     w1s, w1n, w2s, w2n = sum_everywhere(keep, send, core)

time: 178 us -> 171 us (0.961)
  waiting for transfers between devices: 16.8 us -> 6.64 us
  blocking collectives: 36.8 us -> 40.4 us
    pallas_call x1, Pallas kernels: 73.2 us -> 62.1 us  [train(): pl.pallas_call(train_kernel, out_shape=(jax.ShapeDtypeStruct((1, SEEDS),...]
    pallas_call x0 -> x1, Pallas kernels: none -> 10.4 us  [order_positions(): pl.pallas_call(order_kernel, out_shape=jax.ShapeDtypeStruct((POSITIONS, 1...]
    ppermute x3, waiting for transfers between devices: 8.54 us -> 0.01 us  [send_hot(): lax.ppermute(rows[d], 'clique', [(i, (i - d) % 4) for i in range(4)])]
    all_to_all x3, blocking collectives: 36.8 us -> 40.4 us  [exchange(): return lax.all_to_all(x, axes, split_axis=0, concat_axis=0, tiled=True)]
    unnamed x25 -> x23, local copies, waits for them, and re-layouts: 5.84 us -> 5.83 us
  transfers between devices with their start and end apart: 10 -> 10, of which waited for: 8 -> 4; matrix products, arithmetic and copies ran while one was open for 1% -> 1% of each run, Pallas kernels for 2% -> 8%
where the time goes in v3:
time: 171 us
  Pallas kernels  80.1 us (47%)
  blocking collectives  40.4 us (24%)
  starting transfers between devices  36 us (21%)
  local copies, waits for them, and re-layouts  6.73 us (4%)
  waiting for transfers between devices  6.64 us (4%)
    pallas_call x1, Pallas kernels, train(): pl.pallas_call(train_kernel, out_shape=(jax.ShapeDtypeStruct((1, SEEDS),...  62.1 us
    all_to_all x3, blocking collectives, exchange(): return lax.all_to_all(x, axes, split_axis=0, concat_axis=0, tiled=True)  40.4 us
    all_to_all x2, starting transfers between devices, exchange(): return lax.all_to_all(x, axes, split_axis=0, concat_axis=0, tiled=True)  23.6 us
    pallas_call x1, Pallas kernels, order_positions(): pl.pallas_call(order_kernel, out_shape=jax.ShapeDtypeStruct((POSITIONS, 1...  10.4 us
    pallas_call x2, Pallas kernels, pick_rows(): pl.pallas_call(lambda *refs: pick_kernel(n, *refs), out_shape=tuple((jax....  6.69 us
    unnamed x23, local copies, waits for them, and re-layouts  5.83 us
    ppermute x1, starting transfers between devices, sum_everywhere(): other = lax.ppermute(mine, 'core', SWAP)  4.32 us
    ppermute x3, starting transfers between devices, body(): lax.ppermute(hot_asked[d], 'clique', [(i, (i + d) % 4) for i in range(4)])  4.29 us
  transfers between devices with their start and end apart: 10, of which 4 were waited for; matrix products, arithmetic and copies ran while one was open for 1% of the time, Pallas kernels for 8%

profile of v3, /device:TPU:1, one launch (start us, length us, event | category | flops | bytes accessed | tf_op | source)
XLA Modules:
  0.0 170.9 jit_solution(636616074090230795)
XLA Ops:
  0.6 1.4 copy.20
  2.0 13.2 %all-to-all-start = ((s32[64,1,32]{2,1,0:T(1,128)}), s32[64,1,32]{2,1,0:T(1,128)S(1)}, u32[]{:S(2)}, u32[]{:S(2)}) async-start(s32[64,1,32]{2,1,0:T(1,128)} %bitcast.10), calls=%async_computation | async-start | bytes 65536 | tf_op jit(solution)/shard_map/all_to_all | solution.py:350
  15.2 0.9 constant_dynamic-slice_fusion
  16.1 1.3 collective-permute-start
  17.4 1.5 collective-permute-start.2
  18.9 1.5 collective-permute-start.1
  20.4 2.7 %collective-permute-done.1.refs_2_ = s32[512]{0:T(512)S(1)} collective-permute-done((s32[512]{0:T(512)S(1)}, s32[512]{0:T(512)S(1)}, u32[]{:S(2)}, u32[]{:S(2)}) %collective-permute-start.1) | collective-permute-done | bytes 2080 | tf_op jit(solution)/shard_map/ppermute | solution.py:390
  23.1 1.4 all-to-all-done
  24.5 2.2 %copy-done = bf16[16384,128]{1,0:T(8,128)(2,1)S(1)} copy-done((bf16[16384,128]{1,0:T(8,128)(2,1)S(1)}, bf16[16384,128]{1,0:T(8,128)(2,1)}, u32[]{:S(2)}) %copy-start) | copy-done | bytes 4194328
  26.7 3.9 %pick_cold.1 = bf16[64,32,128]{2,1,0:T(8,128)(2,1)} custom-call(s32[64,32]{1,0:T(8,128)S(1)} %bitcast.23, bf16[16384,128]{1,0:T(8,128)(2,1)S(1)} %copy-done), custom_call_target="tpu_custom_call" | custom-call | bytes 4194304 | tf_op jit(solution)/shard_map/pick_cold/pallas_call | solution.py:320
  30.6 0.0 copy-start.5
  30.6 0.0 copy-start.6
  30.7 0.0 copy-start.7
  30.7 0.0 copy-start.8
  30.7 0.0 copy-start.9
  30.7 10.4 %all-to-all-start.1 = ((bf16[64,32,128]{2,1,0:T(8,128)(2,1)}), bf16[64,32,128]{2,1,0:T(8,128)(2,1)S(1)}, u32[]{:S(2)}, u32[]{:S(2)}) async-start(bf16[64,32,128]{2,1,0:T(8,128)(2,1)} %pick_cold.1), calls=%async_computation.1 | async-start | bytes 1048576 | tf_op jit(solution)/shard_map/all_to_all | solution.py:350
  41.2 2.2 %copy-done.1 = bf16[16384,128]{1,0:T(8,128)(2,1)S(1)} copy-done((bf16[16384,128]{1,0:T(8,128)(2,1)S(1)}, bf16[16384,128]{1,0:T(8,128)(2,1)}, u32[]{:S(2)}) %copy-start.1) | copy-done | bytes 4194328
  43.3 2.8 %pick_hot.1 = (bf16[512,128]{1,0:T(8,128)(2,1)S(1)}, bf16[512,128]{1,0:T(8,128)(2,1)S(1)}, bf16[512,128]{1,0:T(8,128)(2,1)S(1)}, bf16[512,128]{1,0:T(8,128)(2,1)S(1)}) custom-call(s32[512]{0:T(512)S(1)} %bitcast.25, s32[512]{0:T(512)S(1)} %collective-permute-done.refs_1_, s32[512]{0:T(512)S(1)} %collective-permute-done.1.refs_2_, ...), custom_call_target="tpu_custom_call" | custom-call | bytes 4194304 | tf_op jit(solution)/shard_map/pick_hot/pallas_call | solution.py:320
  46.1 1.3 collective-permute-start.3
  47.5 0.5 collective-permute-start.4
  48.0 0.6 collective-permute-start.5
  48.6 0.1 pad_add_fusion.where_hot
  48.7 10.4 %order.1.places = s32[11,1,8192]{2,1,0:T(1,128)S(1)} custom-call(s32[15,1,512]{2,1,0:T(1,128)S(1)} %bitcast.24, s32[10,1,7680]{2,1,0:T(1,128)S(1)} %bitcast.22, s32[1,7680]{1,0:T(1,128)S(1)} %copy-done.4), custom_call_target="tpu_custom_call" | custom-call | bytes 8388608 | tf_op jit(solution)/shard_map/order/pallas_call | solution.py:85
  59.2 62.1 %train.1 = (f32[1,512]{1,0:T(1,128)}, f32[640,128]{1,0:T(8,128)S(1)}, f32[640,128]{1,0:T(8,128)S(1)}) custom-call(s32[64]{0:T(128)S(1)} %bitcast.28, s32[4]{0:T(128)S(1)} %pad_add_fusion.where_hot, s32[1]{0:T(128)} %bitcast.5.core, s32[11,1,8192]{2,1,0:T(1,128)S(1)} %order.1.places, bf16[512,128]{1,0:T(8,128)(2,1)S(1)} %get-tuple-element.44.hot0, ...), custom_call_target="tpu_custom_call" | custom-call | flops 4294967296 | bytes 4194304 | tf_op jit(solution)/shard_map/train/pallas_call | solution.py:254
  121.3 1.3 collective-permute-start.6
  122.6 1.3 collective-permute-done.6
  123.9 14.3 %all_to_all.32 = f32[16,5,8,128]{3,2,1,0:T(8,128)S(1)} all-to-all(f32[16,5,8,128]{3,2,1,0:T(8,128)S(1)} %bitcast.29), channel_id=1, replica_groups=mesh['clique'=4,'z'=8,'y'=4,'core'=2] {'clique','y'}, dimensions={0} | all-to-all | bytes 655360 | tf_op jit(solution)/shard_map/all_to_all | solution.py:350
  138.3 14.7 %all_to_all.33 = f32[8,5,8,128]{3,2,1,0:T(8,128)S(1)} all-to-all(f32[8,5,8,128]{3,2,1,0:T(8,128)S(1)} %broadcast_in_dim.7), channel_id=1, replica_groups=mesh['clique'=4,'z'=8,'y'=4,'core'=2] {'z'}, dimensions={0} | all-to-all | bytes 327680 | tf_op jit(solution)/shard_map/all_to_all | solution.py:350
  153.0 11.5 %all_to_all.34 = f32[16,5,8,128]{3,2,1,0:T(8,128)S(1)} all-to-all(f32[16,5,8,128]{3,2,1,0:T(8,128)S(1)} %broadcast_in_dim.8), channel_id=1, replica_groups=mesh['clique'=4,'z'=8,'y'=4,'core'=2] {'clique','y'}, dimensions={0} | all-to-all | bytes 655360 | tf_op jit(solution)/shard_map/all_to_all | solution.py:350
  164.5 4.3 %collective-permute-start.7 = (f32[640,128]{1,0:T(8,128)S(1)}, f32[640,128]{1,0:T(8,128)S(1)}, u32[]{:S(2)}, u32[]{:S(2)}) collective-permute-start(f32[640,128]{1,0:T(8,128)S(1)} %bitcast.20), channel_id=1, source_target_pairs={{0,1},{1,0},{2,3},{3,2},{4,5},{5,4},{6,7},{7,6},{8,9},{9,8},{10,11... | collective-permute-start | bytes 983048 | tf_op jit(solution)/shard_map/ppermute | solution.py:372
  168.8 1.3 collective-permute-done.7.other
  170.1 0.9 split.1
  (26 shorter events, 0.2 us)
Async XLA Ops:
  2.0 22.5 %all-to-all-start = ((s32[64,1,32]{2,1,0:T(1,128)}), s32[64,1,32]{2,1,0:T(1,128)S(1)}, u32[]{:S(2)}, u32[]{:S(2)}) async-start(s32[64,1,32]{2,1,0:T(1,128)} %bitcast.10), calls=%async_computation | async-start | bytes 65536 | tf_op jit(solution)/shard_map/all_to_all | solution.py:350
  16.1 4.3 %collective-permute-start = (s32[512]{0:T(512)S(1)}, s32[512]{0:T(512)S(1)}, u32[]{:S(2)}, u32[]{:S(2)}) collective-permute-start(s32[512]{0:T(512)S(1)} %bitcast.32), channel_id=1, source_target_pairs={{0,64},{64,128},{128,192},{192,0},{1,65},{65,129},{129,193},{193,1... | collective-permute-start | bytes 6152 | tf_op jit(solution)/shard_map/ppermute | solution.py:390
  17.4 3.0 %collective-permute-start.2 = (s32[512]{0:T(512)S(1)}, s32[512]{0:T(512)S(1)}, u32[]{:S(2)}, u32[]{:S(2)}) collective-permute-start(s32[512]{0:T(512)S(1)} %bitcast.31), channel_id=1, source_target_pairs={{0,192},{64,0},{128,64},{192,128},{1,193},{65,1},{129,65},{193,129... | collective-permute-start | bytes 6152 | tf_op jit(solution)/shard_map/ppermute | solution.py:390
  18.9 4.2 %collective-permute-start.1 = (s32[512]{0:T(512)S(1)}, s32[512]{0:T(512)S(1)}, u32[]{:S(2)}, u32[]{:S(2)}) collective-permute-start(s32[512]{0:T(512)S(1)} %bitcast.30), channel_id=1, source_target_pairs={{0,128},{64,192},{128,0},{192,64},{1,129},{65,193},{129,1},{193,65... | collective-permute-start | bytes 6152 | tf_op jit(solution)/shard_map/ppermute | solution.py:390
  24.5 2.2 %copy-start = (bf16[16384,128]{1,0:T(8,128)(2,1)S(1)}, bf16[16384,128]{1,0:T(8,128)(2,1)}, u32[]{:S(2)}) copy-start(bf16[16384,128]{1,0:T(8,128)(2,1)} %refs_1_.1) | copy-start | bytes 12582916
  26.7 22.0 %copy-start.2 = (s32[1,10,7680]{2,0,1:T(1,128)S(1)}, s32[1,10,7680]{2,0,1:T(1,128)}, u32[]{:S(2)}) copy-start(s32[1,10,7680]{2,0,1:T(1,128)} %param.19) | copy-start | bytes 921604
  26.7 22.0 %copy-start.3 = (s32[1,15,512]{2,0,1:T(1,128)S(1)}, s32[1,15,512]{2,0,1:T(1,128)}, u32[]{:S(2)}) copy-start(s32[1,15,512]{2,0,1:T(1,128)} %param.20) | copy-start | bytes 92164
  26.7 22.0 %copy-start.4 = (s32[1,7680]{1,0:T(1,128)S(1)}, s32[1,7680]{1,0:T(1,128)}, u32[]{:S(2)}) copy-start(s32[1,7680]{1,0:T(1,128)} %mid_self.1) | copy-start | bytes 92164
  30.6 28.5 %copy-start.5 = (bf16[256,172]{0,1:T(8,128)(2,1)S(1)}, bf16[256,172]{0,1:T(8,128)(2,1)}, u32[]{:S(2)}) copy-start(bf16[256,172]{0,1:T(8,128)(2,1)} %param.24) | copy-start | bytes 264196
  30.6 28.5 %copy-start.6 = (bf16[256,172]{0,1:T(8,128)(2,1)S(1)}, bf16[256,172]{0,1:T(8,128)(2,1)}, u32[]{:S(2)}) copy-start(bf16[256,172]{0,1:T(8,128)(2,1)} %param.25) | copy-start | bytes 264196
  30.7 28.5 %copy-start.7 = (bf16[128,256]{1,0:T(8,128)(2,1)S(1)}, bf16[128,256]{1,0:T(8,128)(2,1)}, u32[]{:S(2)}) copy-start(bf16[128,256]{1,0:T(8,128)(2,1)} %w1_self.1) | copy-start | bytes 196612
  30.7 28.5 %copy-start.8 = (bf16[128,256]{1,0:T(8,128)(2,1)S(1)}, bf16[128,256]{1,0:T(8,128)(2,1)}, u32[]{:S(2)}) copy-start(bf16[128,256]{1,0:T(8,128)(2,1)} %w1_neigh.1) | copy-start | bytes 196612
  30.7 28.5 %copy-start.9 = (s32[1,512]{1,0:T(1,128)S(1)}, s32[1,512]{1,0:T(1,128)}, u32[]{:S(2)}) copy-start(s32[1,512]{1,0:T(1,128)} %labels.1) | copy-start | bytes 6148
  30.7 28.5 %copy-start.10 = (s32[1,64]{1,0:T(1,128)S(1)}, s32[1,64]{1,0:T(1,128)}, u32[]{:S(2)}) copy-start(s32[1,64]{1,0:T(1,128)} %param.17) | copy-start | bytes 772
  30.7 28.4 %all-to-all-start.1 = ((bf16[64,32,128]{2,1,0:T(8,128)(2,1)}), bf16[64,32,128]{2,1,0:T(8,128)(2,1)S(1)}, u32[]{:S(2)}, u32[]{:S(2)}) async-start(bf16[64,32,128]{2,1,0:T(8,128)(2,1)} %pick_cold.1), calls=%async_computation.1 | async-start | bytes 1048576 | tf_op jit(solution)/shard_map/all_to_all | solution.py:350
  41.2 2.2 %copy-start.1 = (bf16[16384,128]{1,0:T(8,128)(2,1)S(1)}, bf16[16384,128]{1,0:T(8,128)(2,1)}, u32[]{:S(2)}) copy-start(bf16[16384,128]{1,0:T(8,128)(2,1)} %refs_4_.1) | copy-start | bytes 12582916
  46.1 13.0 %collective-permute-start.3 = (bf16[512,128]{1,0:T(8,128)(2,1)S(1)}, bf16[512,128]{1,0:T(8,128)(2,1)S(1)}, u32[]{:S(2)}, u32[]{:S(2)}) collective-permute-start(bf16[512,128]{1,0:T(8,128)(2,1)S(1)} %get-tuple-element.45), channel_id=1, source_target_pairs={{0,192},{64,0},{128,64},{192,128},{1,193},{65,1},{129,65},{193,129... | collective-permute-start | bytes 393224 | tf_op jit(solution)/shard_map/ppermute | solution.py:345
  47.5 11.6 %collective-permute-start.4 = (bf16[512,128]{1,0:T(8,128)(2,1)S(1)}, bf16[512,128]{1,0:T(8,128)(2,1)S(1)}, u32[]{:S(2)}, u32[]{:S(2)}) collective-permute-start(bf16[512,128]{1,0:T(8,128)(2,1)S(1)} %get-tuple-element.46), channel_id=1, source_target_pairs={{0,128},{64,192},{128,0},{192,64},{1,129},{65,193},{129,1},{193,65... | collective-permute-start | bytes 393224 | tf_op jit(solution)/shard_map/ppermute | solution.py:345
  48.0 11.1 %collective-permute-start.5 = (bf16[512,128]{1,0:T(8,128)(2,1)S(1)}, bf16[512,128]{1,0:T(8,128)(2,1)S(1)}, u32[]{:S(2)}, u32[]{:S(2)}) collective-permute-start(bf16[512,128]{1,0:T(8,128)(2,1)S(1)} %get-tuple-element.47), channel_id=1, source_target_pairs={{0,64},{64,128},{128,192},{192,0},{1,65},{65,129},{129,193},{193,1... | collective-permute-start | bytes 393224 | tf_op jit(solution)/shard_map/ppermute | solution.py:345
  121.3 2.6 %collective-permute-start.6 = (f32[640,128]{1,0:T(8,128)S(1)}, f32[640,128]{1,0:T(8,128)S(1)}, u32[]{:S(2)}, u32[]{:S(2)}) collective-permute-start(f32[640,128]{1,0:T(8,128)S(1)} %get-tuple-element.50), channel_id=1, source_target_pairs={{0,1},{1,0},{2,3},{3,2},{4,5},{5,4},{6,7},{7,6},{8,9},{9,8},{10,11... | collective-permute-start | bytes 983048 | tf_op jit(solution)/shard_map/ppermute | solution.py:368
  164.5 5.6 %collective-permute-start.7 = (f32[640,128]{1,0:T(8,128)S(1)}, f32[640,128]{1,0:T(8,128)S(1)}, u32[]{:S(2)}, u32[]{:S(2)}) collective-permute-start(f32[640,128]{1,0:T(8,128)S(1)} %bitcast.20), channel_id=1, source_target_pairs={{0,1},{1,0},{2,3},{3,2},{4,5},{5,4},{6,7},{7,6},{8,9},{9,8},{10,11... | collective-permute-start | bytes 983048 | tf_op jit(solution)/shard_map/ppermute | solution.py:372

commit v4 on v3

--- a/solution.py
+++ b/solution.py
@@ -20,7 +20,8 @@
 FAN1 = 15
 HOT_ROWS = 2048
 COLD_ROWS = 2048
-STEP = 128
+STEP = 64
+FIRST, SECOND = range(32), range(32, STEP)
 SLOTS = SEEDS * (FAN1 + 1)
 CHUNKS = SLOTS // STEP
 SEED_CHUNKS = SEEDS // STEP
@@ -62,22 +63,20 @@
     for copy in copies:
         copy.wait()
 
-    def by_slot(i, carry):
-        base = i * 128
+    chunks = MID // 128
+
+    def by_chunk(i, carry):
+        before = jnp.maximum(i - 1, 0) * 128
+        rows = ordered[pl.ds(pl.multiple_of(before, 128), 128), :].T
+        base = jnp.minimum(i, chunks - 1) * 128
         for u in range(128):
             ordered[pl.ds(base + u, 1), :] = info[pl.ds(slots[base + u], 1), :]
-        return carry
-
-    lax.fori_loop(0, MID // 128, by_slot, 0)
-
-    def by_chunk(i, carry):
-        rows = ordered[pl.ds(pl.multiple_of(i * 128, 128), 128), :].T
-        at = pl.ds(pl.multiple_of(SEEDS + i * 128, 128), 128)
+        at = pl.ds(pl.multiple_of(SEEDS + before, 128), 128)
         for k in range(POSITIONS):
             out[k, :, at] = rows[k : k + 1, :]
         return carry
 
-    lax.fori_loop(0, MID // 128, by_chunk, 0, unroll=4)
+    lax.fori_loop(0, chunks + 1, by_chunk, 0)
 
 
 def order_positions(nbr1, nbr2, mid_self):
@@ -141,9 +140,9 @@
         padded[0:CLASSES, :] = given[...]
     hidden[...] = jnp.zeros((2 * SEEDS, HID), f32)
 
-    def gather(chunk, buffer):
+    def gather(chunk, buffer, part):
         base = chunk * STEP
-        for u in range(STEP):
+        for u in part:
             m = base + u
             rows = [table[pl.ds(near[m], 1), :] for near in neighbours]
             buffer[u : u + 1, 0:F] = table[pl.ds(own[m], 1), :]
@@ -171,11 +170,12 @@
 
     for copy in pieces[0]:
         copy.wait()
-    gather(0, x_even)
+    gather(0, x_even, range(STEP))
 
     def two_chunks(i, carry):
-        gather(2 * i + 1, x_odd)
+        gather(2 * i + 1, x_odd, FIRST)
         forward(2 * i, x_even)
+        gather(2 * i + 1, x_odd, SECOND)
         for p, start in enumerate(PIECES[1:-1]):
 
             @pl.when(2 * i + 2 == start // STEP)
@@ -183,8 +183,9 @@
                 for copy in pieces[p + 1]:
                     copy.wait()
 
-        gather(lax.rem(2 * i + 2, CHUNKS), x_even)
+        gather(lax.rem(2 * i + 2, CHUNKS), x_even, FIRST)
         forward(2 * i + 1, x_odd)
+        gather(lax.rem(2 * i + 2, CHUNKS), x_even, SECOND)
         return carry
 
     lax.fori_loop(0, CHUNKS // 2, two_chunks, 0)

time: 171 us -> 167 us (0.977)
  Pallas kernels: 80.1 us -> 75.7 us
    pallas_call x1, Pallas kernels: 62.1 us -> 59.2 us  [train(): pl.pallas_call(train_kernel, out_shape=(jax.ShapeDtypeStruct((1, SEEDS),...]
  transfers between devices with their start and end apart: 10 -> 10, of which waited for: 4 -> 5; matrix products, arithmetic and copies ran while one was open for 1% -> 1% of each run, Pallas kernels for 8% -> 7%
where the time goes in v4:
time: 167 us
  Pallas kernels  75.7 us (45%)
  blocking collectives  40.2 us (24%)
  starting transfers between devices  35.2 us (21%)
  waiting for transfers between devices  7.77 us (5%)
  local copies, waits for them, and re-layouts  6.73 us (4%)
    pallas_call x1, Pallas kernels, train(): pl.pallas_call(train_kernel, out_shape=(jax.ShapeDtypeStruct((1, SEEDS),...  59.2 us
    all_to_all x3, blocking collectives, exchange(): return lax.all_to_all(x, axes, split_axis=0, concat_axis=0, tiled=True)  40.2 us
    all_to_all x2, starting transfers between devices, exchange(): return lax.all_to_all(x, axes, split_axis=0, concat_axis=0, tiled=True)  23.6 us
    pallas_call x1, Pallas kernels, order_positions(): pl.pallas_call(order_kernel, out_shape=jax.ShapeDtypeStruct((POSITIONS, 1...  9.02 us
    pallas_call x2, Pallas kernels, pick_rows(): pl.pallas_call(lambda *refs: pick_kernel(n, *refs), out_shape=tuple((jax....  6.69 us
    unnamed x23, local copies, waits for them, and re-layouts  5.83 us
    ppermute x1, starting transfers between devices, sum_everywhere(): other = lax.ppermute(mine, 'core', SWAP)  4.32 us
    ppermute x3, starting transfers between devices, body(): lax.ppermute(hot_asked[d], 'clique', [(i, (i + d) % 4) for i in range(4)])  4.29 us
  transfers between devices with their start and end apart: 10, of which 5 were waited for; matrix products, arithmetic and copies ran while one was open for 1% of the time, Pallas kernels for 7%

profile of v4, /device:TPU:1, one launch (start us, length us, event | category | flops | bytes accessed | tf_op | source)
XLA Modules:
  0.0 166.6 jit_solution(4706756000703106083)
XLA Ops:
  0.6 1.4 copy.20
  2.0 13.2 %all-to-all-start = ((s32[64,1,32]{2,1,0:T(1,128)}), s32[64,1,32]{2,1,0:T(1,128)S(1)}, u32[]{:S(2)}, u32[]{:S(2)}) async-start(s32[64,1,32]{2,1,0:T(1,128)} %bitcast.10), calls=%async_computation | async-start | bytes 65536 | tf_op jit(solution)/shard_map/all_to_all | solution.py:351
  15.2 0.9 constant_dynamic-slice_fusion
  16.1 1.3 collective-permute-start
  17.4 1.5 collective-permute-start.2
  18.9 1.5 collective-permute-start.1
  20.4 2.7 %collective-permute-done.1.refs_2_ = s32[512]{0:T(512)S(1)} collective-permute-done((s32[512]{0:T(512)S(1)}, s32[512]{0:T(512)S(1)}, u32[]{:S(2)}, u32[]{:S(2)}) %collective-permute-start.1) | collective-permute-done | bytes 2080 | tf_op jit(solution)/shard_map/ppermute | solution.py:391
  23.1 1.4 all-to-all-done
  24.5 2.2 %copy-done = bf16[16384,128]{1,0:T(8,128)(2,1)S(1)} copy-done((bf16[16384,128]{1,0:T(8,128)(2,1)S(1)}, bf16[16384,128]{1,0:T(8,128)(2,1)}, u32[]{:S(2)}) %copy-start) | copy-done | bytes 4194328
  26.7 3.9 %pick_cold.1 = bf16[64,32,128]{2,1,0:T(8,128)(2,1)} custom-call(s32[64,32]{1,0:T(8,128)S(1)} %bitcast.23, bf16[16384,128]{1,0:T(8,128)(2,1)S(1)} %copy-done), custom_call_target="tpu_custom_call" | custom-call | bytes 4194304 | tf_op jit(solution)/shard_map/pick_cold/pallas_call | solution.py:321
  30.6 0.0 copy-start.5
  30.6 0.0 copy-start.6
  30.7 0.0 copy-start.7
  30.7 0.0 copy-start.8
  30.7 10.4 %all-to-all-start.1 = ((bf16[64,32,128]{2,1,0:T(8,128)(2,1)}), bf16[64,32,128]{2,1,0:T(8,128)(2,1)S(1)}, u32[]{:S(2)}, u32[]{:S(2)}) async-start(bf16[64,32,128]{2,1,0:T(8,128)(2,1)} %pick_cold.1), calls=%async_computation.1 | async-start | bytes 1048576 | tf_op jit(solution)/shard_map/all_to_all | solution.py:351
  41.2 2.2 %copy-done.1 = bf16[16384,128]{1,0:T(8,128)(2,1)S(1)} copy-done((bf16[16384,128]{1,0:T(8,128)(2,1)S(1)}, bf16[16384,128]{1,0:T(8,128)(2,1)}, u32[]{:S(2)}) %copy-start.1) | copy-done | bytes 4194328
  43.3 2.8 %pick_hot.1 = (bf16[512,128]{1,0:T(8,128)(2,1)S(1)}, bf16[512,128]{1,0:T(8,128)(2,1)S(1)}, bf16[512,128]{1,0:T(8,128)(2,1)S(1)}, bf16[512,128]{1,0:T(8,128)(2,1)S(1)}) custom-call(s32[512]{0:T(512)S(1)} %bitcast.25, s32[512]{0:T(512)S(1)} %collective-permute-done.refs_1_, s32[512]{0:T(512)S(1)} %collective-permute-done.1.refs_2_, ...), custom_call_target="tpu_custom_call" | custom-call | bytes 4194304 | tf_op jit(solution)/shard_map/pick_hot/pallas_call | solution.py:321
  46.1 1.3 collective-permute-start.3
  47.5 0.5 collective-permute-start.4
  48.0 0.6 collective-permute-start.5
  48.6 0.1 pad_add_fusion.where_hot
  48.7 9.0 %order.1.places = s32[11,1,8192]{2,1,0:T(1,128)S(1)} custom-call(s32[15,1,512]{2,1,0:T(1,128)S(1)} %bitcast.24, s32[10,1,7680]{2,1,0:T(1,128)S(1)} %bitcast.22, s32[1,7680]{1,0:T(1,128)S(1)} %copy-done.4), custom_call_target="tpu_custom_call" | custom-call | bytes 8388608 | tf_op jit(solution)/shard_map/order/pallas_call | solution.py:84
  57.7 1.1 all-to-all-done.1.cold
  58.9 59.2 %train.1 = (f32[1,512]{1,0:T(1,128)}, f32[640,128]{1,0:T(8,128)S(1)}, f32[640,128]{1,0:T(8,128)S(1)}) custom-call(s32[64]{0:T(128)S(1)} %bitcast.28, s32[4]{0:T(128)S(1)} %pad_add_fusion.where_hot, s32[1]{0:T(128)} %bitcast.5.core, s32[11,1,8192]{2,1,0:T(1,128)S(1)} %order.1.places, bf16[512,128]{1,0:T(8,128)(2,1)S(1)} %get-tuple-element.44.hot0, ...), custom_call_target="tpu_custom_call" | custom-call | flops 4294967296 | bytes 4194304 | tf_op jit(solution)/shard_map/train/pallas_call | solution.py:255
  118.1 0.5 collective-permute-start.6
  118.6 1.3 collective-permute-done.6
  119.9 14.1 %all_to_all.32 = f32[16,5,8,128]{3,2,1,0:T(8,128)S(1)} all-to-all(f32[16,5,8,128]{3,2,1,0:T(8,128)S(1)} %bitcast.29), channel_id=1, replica_groups=mesh['clique'=4,'z'=8,'y'=4,'core'=2] {'clique','y'}, dimensions={0} | all-to-all | bytes 655360 | tf_op jit(solution)/shard_map/all_to_all | solution.py:351
  134.0 14.7 %all_to_all.33 = f32[8,5,8,128]{3,2,1,0:T(8,128)S(1)} all-to-all(f32[8,5,8,128]{3,2,1,0:T(8,128)S(1)} %broadcast_in_dim.7), channel_id=1, replica_groups=mesh['clique'=4,'z'=8,'y'=4,'core'=2] {'z'}, dimensions={0} | all-to-all | bytes 327680 | tf_op jit(solution)/shard_map/all_to_all | solution.py:351
  148.7 11.5 %all_to_all.34 = f32[16,5,8,128]{3,2,1,0:T(8,128)S(1)} all-to-all(f32[16,5,8,128]{3,2,1,0:T(8,128)S(1)} %broadcast_in_dim.8), channel_id=1, replica_groups=mesh['clique'=4,'z'=8,'y'=4,'core'=2] {'clique','y'}, dimensions={0} | all-to-all | bytes 655360 | tf_op jit(solution)/shard_map/all_to_all | solution.py:351
  160.2 4.3 %collective-permute-start.7 = (f32[640,128]{1,0:T(8,128)S(1)}, f32[640,128]{1,0:T(8,128)S(1)}, u32[]{:S(2)}, u32[]{:S(2)}) collective-permute-start(f32[640,128]{1,0:T(8,128)S(1)} %bitcast.20), channel_id=1, source_target_pairs={{0,1},{1,0},{2,3},{3,2},{4,5},{5,4},{6,7},{7,6},{8,9},{9,8},{10,11... | collective-permute-start | bytes 983048 | tf_op jit(solution)/shard_map/ppermute | solution.py:373
  164.5 1.3 collective-permute-done.7.other
  165.7 0.9 split.1
  (26 shorter events, 0.2 us)
Async XLA Ops:
  2.0 22.5 %all-to-all-start = ((s32[64,1,32]{2,1,0:T(1,128)}), s32[64,1,32]{2,1,0:T(1,128)S(1)}, u32[]{:S(2)}, u32[]{:S(2)}) async-start(s32[64,1,32]{2,1,0:T(1,128)} %bitcast.10), calls=%async_computation | async-start | bytes 65536 | tf_op jit(solution)/shard_map/all_to_all | solution.py:351
  16.1 4.3 %collective-permute-start = (s32[512]{0:T(512)S(1)}, s32[512]{0:T(512)S(1)}, u32[]{:S(2)}, u32[]{:S(2)}) collective-permute-start(s32[512]{0:T(512)S(1)} %bitcast.32), channel_id=1, source_target_pairs={{0,64},{64,128},{128,192},{192,0},{1,65},{65,129},{129,193},{193,1... | collective-permute-start | bytes 6152 | tf_op jit(solution)/shard_map/ppermute | solution.py:391
  17.4 3.0 %collective-permute-start.2 = (s32[512]{0:T(512)S(1)}, s32[512]{0:T(512)S(1)}, u32[]{:S(2)}, u32[]{:S(2)}) collective-permute-start(s32[512]{0:T(512)S(1)} %bitcast.31), channel_id=1, source_target_pairs={{0,192},{64,0},{128,64},{192,128},{1,193},{65,1},{129,65},{193,129... | collective-permute-start | bytes 6152 | tf_op jit(solution)/shard_map/ppermute | solution.py:391
  18.9 4.2 %collective-permute-start.1 = (s32[512]{0:T(512)S(1)}, s32[512]{0:T(512)S(1)}, u32[]{:S(2)}, u32[]{:S(2)}) collective-permute-start(s32[512]{0:T(512)S(1)} %bitcast.30), channel_id=1, source_target_pairs={{0,128},{64,192},{128,0},{192,64},{1,129},{65,193},{129,1},{193,65... | collective-permute-start | bytes 6152 | tf_op jit(solution)/shard_map/ppermute | solution.py:391
  24.5 2.2 %copy-start = (bf16[16384,128]{1,0:T(8,128)(2,1)S(1)}, bf16[16384,128]{1,0:T(8,128)(2,1)}, u32[]{:S(2)}) copy-start(bf16[16384,128]{1,0:T(8,128)(2,1)} %refs_1_.1) | copy-start | bytes 12582916
  26.7 22.0 %copy-start.2 = (s32[1,10,7680]{2,0,1:T(1,128)S(1)}, s32[1,10,7680]{2,0,1:T(1,128)}, u32[]{:S(2)}) copy-start(s32[1,10,7680]{2,0,1:T(1,128)} %param.19) | copy-start | bytes 921604
  26.7 22.0 %copy-start.3 = (s32[1,15,512]{2,0,1:T(1,128)S(1)}, s32[1,15,512]{2,0,1:T(1,128)}, u32[]{:S(2)}) copy-start(s32[1,15,512]{2,0,1:T(1,128)} %param.20) | copy-start | bytes 92164
  26.7 22.0 %copy-start.4 = (s32[1,7680]{1,0:T(1,128)S(1)}, s32[1,7680]{1,0:T(1,128)}, u32[]{:S(2)}) copy-start(s32[1,7680]{1,0:T(1,128)} %mid_self.1) | copy-start | bytes 92164
  30.6 28.2 %copy-start.5 = (bf16[256,172]{0,1:T(8,128)(2,1)S(1)}, bf16[256,172]{0,1:T(8,128)(2,1)}, u32[]{:S(2)}) copy-start(bf16[256,172]{0,1:T(8,128)(2,1)} %param.24) | copy-start | bytes 264196
  30.6 28.2 %copy-start.6 = (bf16[256,172]{0,1:T(8,128)(2,1)S(1)}, bf16[256,172]{0,1:T(8,128)(2,1)}, u32[]{:S(2)}) copy-start(bf16[256,172]{0,1:T(8,128)(2,1)} %param.25) | copy-start | bytes 264196
  30.7 28.2 %copy-start.7 = (bf16[128,256]{1,0:T(8,128)(2,1)S(1)}, bf16[128,256]{1,0:T(8,128)(2,1)}, u32[]{:S(2)}) copy-start(bf16[128,256]{1,0:T(8,128)(2,1)} %w1_self.1) | copy-start | bytes 196612
  30.7 28.2 %copy-start.8 = (bf16[128,256]{1,0:T(8,128)(2,1)S(1)}, bf16[128,256]{1,0:T(8,128)(2,1)}, u32[]{:S(2)}) copy-start(bf16[128,256]{1,0:T(8,128)(2,1)} %w1_neigh.1) | copy-start | bytes 196612
  30.7 28.2 %copy-start.9 = (s32[1,512]{1,0:T(1,128)S(1)}, s32[1,512]{1,0:T(1,128)}, u32[]{:S(2)}) copy-start(s32[1,512]{1,0:T(1,128)} %labels.1) | copy-start | bytes 6148
  30.7 28.2 %copy-start.10 = (s32[1,64]{1,0:T(1,128)S(1)}, s32[1,64]{1,0:T(1,128)}, u32[]{:S(2)}) copy-start(s32[1,64]{1,0:T(1,128)} %param.17) | copy-start | bytes 772
  30.7 28.2 %all-to-all-start.1 = ((bf16[64,32,128]{2,1,0:T(8,128)(2,1)}), bf16[64,32,128]{2,1,0:T(8,128)(2,1)S(1)}, u32[]{:S(2)}, u32[]{:S(2)}) async-start(bf16[64,32,128]{2,1,0:T(8,128)(2,1)} %pick_cold.1), calls=%async_computation.1 | async-start | bytes 1048576 | tf_op jit(solution)/shard_map/all_to_all | solution.py:351
  41.2 2.2 %copy-start.1 = (bf16[16384,128]{1,0:T(8,128)(2,1)S(1)}, bf16[16384,128]{1,0:T(8,128)(2,1)}, u32[]{:S(2)}) copy-start(bf16[16384,128]{1,0:T(8,128)(2,1)} %refs_4_.1) | copy-start | bytes 12582916
  46.1 11.6 %collective-permute-start.3 = (bf16[512,128]{1,0:T(8,128)(2,1)S(1)}, bf16[512,128]{1,0:T(8,128)(2,1)S(1)}, u32[]{:S(2)}, u32[]{:S(2)}) collective-permute-start(bf16[512,128]{1,0:T(8,128)(2,1)S(1)} %get-tuple-element.45), channel_id=1, source_target_pairs={{0,192},{64,0},{128,64},{192,128},{1,193},{65,1},{129,65},{193,129... | collective-permute-start | bytes 393224 | tf_op jit(solution)/shard_map/ppermute | solution.py:346
  47.5 10.3 %collective-permute-start.4 = (bf16[512,128]{1,0:T(8,128)(2,1)S(1)}, bf16[512,128]{1,0:T(8,128)(2,1)S(1)}, u32[]{:S(2)}, u32[]{:S(2)}) collective-permute-start(bf16[512,128]{1,0:T(8,128)(2,1)S(1)} %get-tuple-element.46), channel_id=1, source_target_pairs={{0,128},{64,192},{128,0},{192,64},{1,129},{65,193},{129,1},{193,65... | collective-permute-start | bytes 393224 | tf_op jit(solution)/shard_map/ppermute | solution.py:346
  48.0 9.7 %collective-permute-start.5 = (bf16[512,128]{1,0:T(8,128)(2,1)S(1)}, bf16[512,128]{1,0:T(8,128)(2,1)S(1)}, u32[]{:S(2)}, u32[]{:S(2)}) collective-permute-start(bf16[512,128]{1,0:T(8,128)(2,1)S(1)} %get-tuple-element.47), channel_id=1, source_target_pairs={{0,64},{64,128},{128,192},{192,0},{1,65},{65,129},{129,193},{193,1... | collective-permute-start | bytes 393224 | tf_op jit(solution)/shard_map/ppermute | solution.py:346
  118.1 1.7 %collective-permute-start.6 = (f32[640,128]{1,0:T(8,128)S(1)}, f32[640,128]{1,0:T(8,128)S(1)}, u32[]{:S(2)}, u32[]{:S(2)}) collective-permute-start(f32[640,128]{1,0:T(8,128)S(1)} %get-tuple-element.50), channel_id=1, source_target_pairs={{0,1},{1,0},{2,3},{3,2},{4,5},{5,4},{6,7},{7,6},{8,9},{9,8},{10,11... | collective-permute-start | bytes 983048 | tf_op jit(solution)/shard_map/ppermute | solution.py:369
  160.2 5.6 %collective-permute-start.7 = (f32[640,128]{1,0:T(8,128)S(1)}, f32[640,128]{1,0:T(8,128)S(1)}, u32[]{:S(2)}, u32[]{:S(2)}) collective-permute-start(f32[640,128]{1,0:T(8,128)S(1)} %bitcast.20), channel_id=1, source_target_pairs={{0,1},{1,0},{2,3},{3,2},{4,5},{5,4},{6,7},{7,6},{8,9},{9,8},{10,11... | collective-permute-start | bytes 983048 | tf_op jit(solution)/shard_map/ppermute | solution.py:373

commit v5 on v4

--- a/solution.py
+++ b/solution.py
@@ -27,7 +27,7 @@
 SEED_CHUNKS = SEEDS // STEP
 HALF_ROWS = 640
 PARTS = 8
-PIECES = (0, 512, 2048, SLOTS)
+PIECES = (0, 128, 1024, SLOTS)
 GELU_C = float(np.sqrt(2.0 / np.pi))
 GELU_A = 0.044715
 
@@ -289,18 +289,11 @@
 
 def pick_kernel(n, *refs):
     asked, shard, given = refs[:n], refs[n], refs[n + 1 : 2 * n + 1]
-    narrow, wide, picked, copied = refs[2 * n + 1 :]
+    wide, picked = refs[2 * n + 1 :]
     step = shard.shape[0] // PARTS
-    parts = [pl.ds(i * step, step) for i in range(PARTS)]
-    copies = [
-        pltpu.make_async_copy(shard.at[part], narrow.at[part], copied.at[i])
-        for i, part in enumerate(parts)
-    ]
-    for copy in copies:
-        copy.start()
-    for copy, part in zip(copies, parts):
-        copy.wait()
-        wide[part, :] = narrow[part, :].astype(jnp.float32)
+    for i in range(PARTS):
+        part = pl.ds(i * step, step)
+        wide[part, :] = shard[part, :].astype(jnp.float32)
     row = 0
     for ids, out in zip(asked, given):
         first = row
@@ -321,15 +314,13 @@
     return pl.pallas_call(
         lambda *refs: pick_kernel(n, *refs),
         out_shape=tuple(jax.ShapeDtypeStruct(ids.shape + (F,), jnp.bfloat16) for ids in asked),
-        in_specs=[pl.BlockSpec(memory_space=pltpu.SMEM)] * n + [pl.BlockSpec(memory_space=pltpu.HBM)],
+        in_specs=[pl.BlockSpec(memory_space=pltpu.SMEM)] * n + [pl.BlockSpec(memory_space=pltpu.VMEM)],
         out_specs=tuple(pl.BlockSpec(memory_space=pltpu.VMEM) for _ in asked),
         scratch_shapes=[
-            pltpu.VMEM(shard.shape, shard.dtype),
             pltpu.VMEM(shard.shape, jnp.float32),
             pltpu.VMEM((total, F), jnp.float32),
-            pltpu.SemaphoreType.DMA((PARTS,)),
         ],
-        compiler_params=pltpu.CompilerParams(vmem_limit_bytes=40 << 20),
+        compiler_params=pltpu.CompilerParams(vmem_limit_bytes=24 << 20),
         cost_estimate=pl.CostEstimate(flops=0, bytes_accessed=4 << 20, transcendentals=0),
         name=name,
     )(*asked, shard)

time: 167 us -> 166 us (level)
  no operation moved by 1% of the time
where the time goes in v5:
time: 166 us
  Pallas kernels  74.7 us (45%)
  blocking collectives  39.9 us (24%)
  starting transfers between devices  35.1 us (21%)
  waiting for transfers between devices  8.15 us (5%)
  local copies, waits for them, and re-layouts  6.72 us (4%)
    pallas_call x1, Pallas kernels, train(): pl.pallas_call(train_kernel, out_shape=(jax.ShapeDtypeStruct((1, SEEDS),...  58.9 us
    all_to_all x3, blocking collectives, exchange(): return lax.all_to_all(x, axes, split_axis=0, concat_axis=0, tiled=True)  39.9 us
    all_to_all x2, starting transfers between devices, exchange(): return lax.all_to_all(x, axes, split_axis=0, concat_axis=0, tiled=True)  23.6 us
    pallas_call x1, Pallas kernels, order_positions(): pl.pallas_call(order_kernel, out_shape=jax.ShapeDtypeStruct((POSITIONS, 1...  9.02 us
    pallas_call x2, Pallas kernels, pick_rows(): pl.pallas_call(lambda *refs: pick_kernel(n, *refs), out_shape=tuple((jax....  5.93 us
    unnamed x23, local copies, waits for them, and re-layouts  5.82 us
    ppermute x1, starting transfers between devices, sum_everywhere(): other = lax.ppermute(mine, 'core', SWAP)  4.32 us
    ppermute x3, starting transfers between devices, body(): lax.ppermute(hot_asked[d], 'clique', [(i, (i + d) % 4) for i in range(4)])  4.29 us
  transfers between devices with their start and end apart: 10, of which 5 were waited for; matrix products, arithmetic and copies ran while one was open for 1% of the time, Pallas kernels for 7%

profile of v5, /device:TPU:1, one launch (start us, length us, event | category | flops | bytes accessed | tf_op | source)
XLA Modules:
  0.0 165.5 jit_solution(7978956378642226694)
XLA Ops:
  0.6 1.4 copy.20
  2.0 13.2 %all-to-all-start = ((s32[64,1,32]{2,1,0:T(1,128)}), s32[64,1,32]{2,1,0:T(1,128)S(1)}, u32[]{:S(2)}, u32[]{:S(2)}) async-start(s32[64,1,32]{2,1,0:T(1,128)} %bitcast.10), calls=%async_computation | async-start | bytes 65536 | tf_op jit(solution)/shard_map/all_to_all | solution.py:342
  15.2 0.9 constant_dynamic-slice_fusion
  16.1 1.3 collective-permute-start
  17.4 1.5 collective-permute-start.2
  18.9 1.5 collective-permute-start.1
  20.4 0.0 collective-permute-done.refs_1_
  20.4 2.7 %collective-permute-done.1.refs_2_ = s32[512]{0:T(512)S(1)} collective-permute-done((s32[512]{0:T(512)S(1)}, s32[512]{0:T(512)S(1)}, u32[]{:S(2)}, u32[]{:S(2)}) %collective-permute-start.1) | collective-permute-done | bytes 2080 | tf_op jit(solution)/shard_map/ppermute | solution.py:382
  23.1 1.4 all-to-all-done
  24.5 2.2 %copy-done = bf16[16384,128]{1,0:T(8,128)(2,1)S(1)} copy-done((bf16[16384,128]{1,0:T(8,128)(2,1)S(1)}, bf16[16384,128]{1,0:T(8,128)(2,1)}, u32[]{:S(2)}) %copy-start) | copy-done | bytes 4194328
  26.7 3.5 %pick_cold.1 = bf16[64,32,128]{2,1,0:T(8,128)(2,1)} custom-call(s32[64,32]{1,0:T(8,128)S(1)} %bitcast.23, bf16[16384,128]{1,0:T(8,128)(2,1)S(1)} %copy-done), custom_call_target="tpu_custom_call" | custom-call | bytes 4194304 | tf_op jit(solution)/shard_map/pick_cold/pallas_call | solution.py:314
  30.3 0.0 copy-start.9
  30.3 0.0 copy-start.10
  30.3 10.4 %all-to-all-start.1 = ((bf16[64,32,128]{2,1,0:T(8,128)(2,1)}), bf16[64,32,128]{2,1,0:T(8,128)(2,1)S(1)}, u32[]{:S(2)}, u32[]{:S(2)}) async-start(bf16[64,32,128]{2,1,0:T(8,128)(2,1)} %pick_cold.1), calls=%async_computation.1 | async-start | bytes 1048576 | tf_op jit(solution)/shard_map/all_to_all | solution.py:342
  40.7 0.0 copy-start.1
  40.7 2.2 %copy-done.1 = bf16[16384,128]{1,0:T(8,128)(2,1)S(1)} copy-done((bf16[16384,128]{1,0:T(8,128)(2,1)S(1)}, bf16[16384,128]{1,0:T(8,128)(2,1)}, u32[]{:S(2)}) %copy-start.1) | copy-done | bytes 4194328
  42.9 2.4 %pick_hot.1 = (bf16[512,128]{1,0:T(8,128)(2,1)S(1)}, bf16[512,128]{1,0:T(8,128)(2,1)S(1)}, bf16[512,128]{1,0:T(8,128)(2,1)S(1)}, bf16[512,128]{1,0:T(8,128)(2,1)S(1)}) custom-call(s32[512]{0:T(512)S(1)} %bitcast.25, s32[512]{0:T(512)S(1)} %collective-permute-done.refs_1_, s32[512]{0:T(512)S(1)} %collective-permute-done.1.refs_2_, ...), custom_call_target="tpu_custom_call" | custom-call | bytes 4194304 | tf_op jit(solution)/shard_map/pick_hot/pallas_call | solution.py:314
  45.3 1.3 collective-permute-start.3
  46.7 0.5 collective-permute-start.4
  47.2 0.6 collective-permute-start.5
  47.8 0.1 pad_add_fusion.where_hot
  47.9 9.0 %order.1.places = s32[11,1,8192]{2,1,0:T(1,128)S(1)} custom-call(s32[15,1,512]{2,1,0:T(1,128)S(1)} %bitcast.24, s32[10,1,7680]{2,1,0:T(1,128)S(1)} %bitcast.22, s32[1,7680]{1,0:T(1,128)S(1)} %copy-done.4), custom_call_target="tpu_custom_call" | custom-call | bytes 8388608 | tf_op jit(solution)/shard_map/order/pallas_call | solution.py:84
  56.9 1.5 all-to-all-done.1.cold
  58.5 58.9 %train.1 = (f32[1,512]{1,0:T(1,128)}, f32[640,128]{1,0:T(8,128)S(1)}, f32[640,128]{1,0:T(8,128)S(1)}) custom-call(s32[64]{0:T(128)S(1)} %bitcast.28, s32[4]{0:T(128)S(1)} %pad_add_fusion.where_hot, s32[1]{0:T(128)} %bitcast.5.core, s32[11,1,8192]{2,1,0:T(1,128)S(1)} %order.1.places, bf16[512,128]{1,0:T(8,128)(2,1)S(1)} %get-tuple-element.44.hot0, ...), custom_call_target="tpu_custom_call" | custom-call | flops 4294967296 | bytes 4194304 | tf_op jit(solution)/shard_map/train/pallas_call | solution.py:255
  117.4 0.5 collective-permute-start.6
  117.8 1.3 collective-permute-done.6
  119.1 13.7 %all_to_all.32 = f32[16,5,8,128]{3,2,1,0:T(8,128)S(1)} all-to-all(f32[16,5,8,128]{3,2,1,0:T(8,128)S(1)} %bitcast.29), channel_id=1, replica_groups=mesh['clique'=4,'z'=8,'y'=4,'core'=2] {'clique','y'}, dimensions={0} | all-to-all | bytes 655360 | tf_op jit(solution)/shard_map/all_to_all | solution.py:342
  132.9 14.7 %all_to_all.33 = f32[8,5,8,128]{3,2,1,0:T(8,128)S(1)} all-to-all(f32[8,5,8,128]{3,2,1,0:T(8,128)S(1)} %broadcast_in_dim.7), channel_id=1, replica_groups=mesh['clique'=4,'z'=8,'y'=4,'core'=2] {'z'}, dimensions={0} | all-to-all | bytes 327680 | tf_op jit(solution)/shard_map/all_to_all | solution.py:342
  147.6 11.5 %all_to_all.34 = f32[16,5,8,128]{3,2,1,0:T(8,128)S(1)} all-to-all(f32[16,5,8,128]{3,2,1,0:T(8,128)S(1)} %broadcast_in_dim.8), channel_id=1, replica_groups=mesh['clique'=4,'z'=8,'y'=4,'core'=2] {'clique','y'}, dimensions={0} | all-to-all | bytes 655360 | tf_op jit(solution)/shard_map/all_to_all | solution.py:342
  159.1 4.3 %collective-permute-start.7 = (f32[640,128]{1,0:T(8,128)S(1)}, f32[640,128]{1,0:T(8,128)S(1)}, u32[]{:S(2)}, u32[]{:S(2)}) collective-permute-start(f32[640,128]{1,0:T(8,128)S(1)} %bitcast.20), channel_id=1, source_target_pairs={{0,1},{1,0},{2,3},{3,2},{4,5},{5,4},{6,7},{7,6},{8,9},{9,8},{10,11... | collective-permute-start | bytes 983048 | tf_op jit(solution)/shard_map/ppermute | solution.py:364
  163.4 1.3 collective-permute-done.7.other
  164.7 0.9 split.1
  (26 shorter events, 0.2 us)
Async XLA Ops:
  2.0 22.5 %all-to-all-start = ((s32[64,1,32]{2,1,0:T(1,128)}), s32[64,1,32]{2,1,0:T(1,128)S(1)}, u32[]{:S(2)}, u32[]{:S(2)}) async-start(s32[64,1,32]{2,1,0:T(1,128)} %bitcast.10), calls=%async_computation | async-start | bytes 65536 | tf_op jit(solution)/shard_map/all_to_all | solution.py:342
  16.1 4.3 %collective-permute-start = (s32[512]{0:T(512)S(1)}, s32[512]{0:T(512)S(1)}, u32[]{:S(2)}, u32[]{:S(2)}) collective-permute-start(s32[512]{0:T(512)S(1)} %bitcast.32), channel_id=1, source_target_pairs={{0,64},{64,128},{128,192},{192,0},{1,65},{65,129},{129,193},{193,1... | collective-permute-start | bytes 6152 | tf_op jit(solution)/shard_map/ppermute | solution.py:382
  17.4 3.0 %collective-permute-start.2 = (s32[512]{0:T(512)S(1)}, s32[512]{0:T(512)S(1)}, u32[]{:S(2)}, u32[]{:S(2)}) collective-permute-start(s32[512]{0:T(512)S(1)} %bitcast.31), channel_id=1, source_target_pairs={{0,192},{64,0},{128,64},{192,128},{1,193},{65,1},{129,65},{193,129... | collective-permute-start | bytes 6152 | tf_op jit(solution)/shard_map/ppermute | solution.py:382
  18.9 4.2 %collective-permute-start.1 = (s32[512]{0:T(512)S(1)}, s32[512]{0:T(512)S(1)}, u32[]{:S(2)}, u32[]{:S(2)}) collective-permute-start(s32[512]{0:T(512)S(1)} %bitcast.30), channel_id=1, source_target_pairs={{0,128},{64,192},{128,0},{192,64},{1,129},{65,193},{129,1},{193,65... | collective-permute-start | bytes 6152 | tf_op jit(solution)/shard_map/ppermute | solution.py:382
  24.5 2.2 %copy-start = (bf16[16384,128]{1,0:T(8,128)(2,1)S(1)}, bf16[16384,128]{1,0:T(8,128)(2,1)}, u32[]{:S(2)}) copy-start(bf16[16384,128]{1,0:T(8,128)(2,1)} %refs_1_.1) | copy-start | bytes 12582916
  26.7 21.2 %copy-start.2 = (s32[1,10,7680]{2,0,1:T(1,128)S(1)}, s32[1,10,7680]{2,0,1:T(1,128)}, u32[]{:S(2)}) copy-start(s32[1,10,7680]{2,0,1:T(1,128)} %param.19) | copy-start | bytes 921604
  26.7 21.2 %copy-start.3 = (s32[1,15,512]{2,0,1:T(1,128)S(1)}, s32[1,15,512]{2,0,1:T(1,128)}, u32[]{:S(2)}) copy-start(s32[1,15,512]{2,0,1:T(1,128)} %param.20) | copy-start | bytes 92164
  26.7 21.2 %copy-start.4 = (s32[1,7680]{1,0:T(1,128)S(1)}, s32[1,7680]{1,0:T(1,128)}, u32[]{:S(2)}) copy-start(s32[1,7680]{1,0:T(1,128)} %mid_self.1) | copy-start | bytes 92164
  30.2 28.2 %copy-start.5 = (bf16[256,172]{0,1:T(8,128)(2,1)S(1)}, bf16[256,172]{0,1:T(8,128)(2,1)}, u32[]{:S(2)}) copy-start(bf16[256,172]{0,1:T(8,128)(2,1)} %param.24) | copy-start | bytes 264196
  30.2 28.2 %copy-start.6 = (bf16[256,172]{0,1:T(8,128)(2,1)S(1)}, bf16[256,172]{0,1:T(8,128)(2,1)}, u32[]{:S(2)}) copy-start(bf16[256,172]{0,1:T(8,128)(2,1)} %param.25) | copy-start | bytes 264196
  30.3 28.2 %copy-start.7 = (bf16[128,256]{1,0:T(8,128)(2,1)S(1)}, bf16[128,256]{1,0:T(8,128)(2,1)}, u32[]{:S(2)}) copy-start(bf16[128,256]{1,0:T(8,128)(2,1)} %w1_self.1) | copy-start | bytes 196612
  30.3 28.2 %copy-start.8 = (bf16[128,256]{1,0:T(8,128)(2,1)S(1)}, bf16[128,256]{1,0:T(8,128)(2,1)}, u32[]{:S(2)}) copy-start(bf16[128,256]{1,0:T(8,128)(2,1)} %w1_neigh.1) | copy-start | bytes 196612
  30.3 28.2 %copy-start.9 = (s32[1,512]{1,0:T(1,128)S(1)}, s32[1,512]{1,0:T(1,128)}, u32[]{:S(2)}) copy-start(s32[1,512]{1,0:T(1,128)} %labels.1) | copy-start | bytes 6148
  30.3 28.2 %copy-start.10 = (s32[1,64]{1,0:T(1,128)S(1)}, s32[1,64]{1,0:T(1,128)}, u32[]{:S(2)}) copy-start(s32[1,64]{1,0:T(1,128)} %param.17) | copy-start | bytes 772
  30.3 28.2 %all-to-all-start.1 = ((bf16[64,32,128]{2,1,0:T(8,128)(2,1)}), bf16[64,32,128]{2,1,0:T(8,128)(2,1)S(1)}, u32[]{:S(2)}, u32[]{:S(2)}) async-start(bf16[64,32,128]{2,1,0:T(8,128)(2,1)} %pick_cold.1), calls=%async_computation.1 | async-start | bytes 1048576 | tf_op jit(solution)/shard_map/all_to_all | solution.py:342
  40.7 2.2 %copy-start.1 = (bf16[16384,128]{1,0:T(8,128)(2,1)S(1)}, bf16[16384,128]{1,0:T(8,128)(2,1)}, u32[]{:S(2)}) copy-start(bf16[16384,128]{1,0:T(8,128)(2,1)} %refs_4_.1) | copy-start | bytes 12582916
  45.3 11.6 %collective-permute-start.3 = (bf16[512,128]{1,0:T(8,128)(2,1)S(1)}, bf16[512,128]{1,0:T(8,128)(2,1)S(1)}, u32[]{:S(2)}, u32[]{:S(2)}) collective-permute-start(bf16[512,128]{1,0:T(8,128)(2,1)S(1)} %get-tuple-element.45), channel_id=1, source_target_pairs={{0,192},{64,0},{128,64},{192,128},{1,193},{65,1},{129,65},{193,129... | collective-permute-start | bytes 393224 | tf_op jit(solution)/shard_map/ppermute | solution.py:337
  46.7 10.3 %collective-permute-start.4 = (bf16[512,128]{1,0:T(8,128)(2,1)S(1)}, bf16[512,128]{1,0:T(8,128)(2,1)S(1)}, u32[]{:S(2)}, u32[]{:S(2)}) collective-permute-start(bf16[512,128]{1,0:T(8,128)(2,1)S(1)} %get-tuple-element.46), channel_id=1, source_target_pairs={{0,128},{64,192},{128,0},{192,64},{1,129},{65,193},{129,1},{193,65... | collective-permute-start | bytes 393224 | tf_op jit(solution)/shard_map/ppermute | solution.py:337
  47.2 9.7 %collective-permute-start.5 = (bf16[512,128]{1,0:T(8,128)(2,1)S(1)}, bf16[512,128]{1,0:T(8,128)(2,1)S(1)}, u32[]{:S(2)}, u32[]{:S(2)}) collective-permute-start(bf16[512,128]{1,0:T(8,128)(2,1)S(1)} %get-tuple-element.47), channel_id=1, source_target_pairs={{0,64},{64,128},{128,192},{192,0},{1,65},{65,129},{129,193},{193,1... | collective-permute-start | bytes 393224 | tf_op jit(solution)/shard_map/ppermute | solution.py:337
  117.4 1.7 %collective-permute-start.6 = (f32[640,128]{1,0:T(8,128)S(1)}, f32[640,128]{1,0:T(8,128)S(1)}, u32[]{:S(2)}, u32[]{:S(2)}) collective-permute-start(f32[640,128]{1,0:T(8,128)S(1)} %get-tuple-element.50), channel_id=1, source_target_pairs={{0,1},{1,0},{2,3},{3,2},{4,5},{5,4},{6,7},{7,6},{8,9},{9,8},{10,11... | collective-permute-start | bytes 983048 | tf_op jit(solution)/shard_map/ppermute | solution.py:360
  159.1 5.6 %collective-permute-start.7 = (f32[640,128]{1,0:T(8,128)S(1)}, f32[640,128]{1,0:T(8,128)S(1)}, u32[]{:S(2)}, u32[]{:S(2)}) collective-permute-start(f32[640,128]{1,0:T(8,128)S(1)} %bitcast.20), channel_id=1, source_target_pairs={{0,1},{1,0},{2,3},{3,2},{4,5},{5,4},{6,7},{7,6},{8,9},{9,8},{10,11... | collective-permute-start | bytes 983048 | tf_op jit(solution)/shard_map/ppermute | solution.py:364

commit v6 on v5

--- a/solution.py
+++ b/solution.py
@@ -56,7 +56,7 @@
         info[at, :] = jnp.concatenate([*rows, empty], axis=0).T
         return carry
 
-    lax.fori_loop(0, MID // 128, by_node, 0, unroll=4)
+    lax.fori_loop(0, MID // 128, by_node, 0, unroll=10)
     for k in range(FAN0):
         out[k, :, 0:SEEDS] = nbr1[k, :, 0:SEEDS]
     out[FAN0, :, 0:SEEDS] = mid_self[:, 0:SEEDS]
@@ -237,11 +237,11 @@
     w1_acc[...] = backward(0, slice(0, SEEDS))
 
     def add_block(j, carry):
-        terms_of = [backward(5 * j + 1 + i, slice(SEEDS, 2 * SEEDS)) for i in range(5)]
+        terms_of = [backward(15 * j + 1 + i, slice(SEEDS, 2 * SEEDS)) for i in range(15)]
         w1_acc[...] += tree_sum(terms_of)
         return carry
 
-    lax.fori_loop(0, FAN1 // 5, add_block, 0)
+    lax.fori_loop(0, FAN1 // 15, add_block, 0)
     terms[left, 0:256, :] = w1_acc[:, 0:F]
     terms[right, 0:256, :] = w1_acc[:, F:]
     keep_out[...] = terms[0]

time: 166 us -> 165 us (level)
  transfers between devices with their start and end apart: 10 -> 10, of which waited for: 5 -> 6; matrix products, arithmetic and copies ran while one was open for 1% -> 1% of each run, Pallas kernels for 7% -> 7%
where the time goes in v6:
time: 165 us
  Pallas kernels  74.1 us (45%)
  blocking collectives  39.2 us (24%)
  starting transfers between devices  35.2 us (21%)
  waiting for transfers between devices  8.78 us (5%)
  local copies, waits for them, and re-layouts  6.72 us (4%)
    pallas_call x1, Pallas kernels, train(): pl.pallas_call(train_kernel, out_shape=(jax.ShapeDtypeStruct((1, SEEDS),...  58.9 us
    all_to_all x3, blocking collectives, exchange(): return lax.all_to_all(x, axes, split_axis=0, concat_axis=0, tiled=True)  39.2 us
    all_to_all x2, starting transfers between devices, exchange(): return lax.all_to_all(x, axes, split_axis=0, concat_axis=0, tiled=True)  23.6 us
    pallas_call x1, Pallas kernels, order_positions(): pl.pallas_call(order_kernel, out_shape=jax.ShapeDtypeStruct((POSITIONS, 1...  8.41 us
    pallas_call x2, Pallas kernels, pick_rows(): pl.pallas_call(lambda *refs: pick_kernel(n, *refs), out_shape=tuple((jax....  5.93 us
    unnamed x23, local copies, waits for them, and re-layouts  5.82 us
    ppermute x1, starting transfers between devices, sum_everywhere(): other = lax.ppermute(mine, 'core', SWAP)  4.32 us
    ppermute x3, starting transfers between devices, body(): lax.ppermute(hot_asked[d], 'clique', [(i, (i + d) % 4) for i in range(4)])  4.29 us
  transfers between devices with their start and end apart: 10, of which 6 were waited for; matrix products, arithmetic and copies ran while one was open for 1% of the time, Pallas kernels for 7%

profile of v6, /device:TPU:1, one launch (start us, length us, event | category | flops | bytes accessed | tf_op | source)
XLA Modules:
  0.0 165.0 jit_solution(9131473369672299764)
XLA Ops:
  0.6 1.4 copy.20
  2.0 13.2 %all-to-all-start = ((s32[64,1,32]{2,1,0:T(1,128)}), s32[64,1,32]{2,1,0:T(1,128)S(1)}, u32[]{:S(2)}, u32[]{:S(2)}) async-start(s32[64,1,32]{2,1,0:T(1,128)} %bitcast.10), calls=%async_computation | async-start | bytes 65536 | tf_op jit(solution)/shard_map/all_to_all | solution.py:342
  15.2 0.9 constant_dynamic-slice_fusion
  16.1 1.3 collective-permute-start
  17.4 1.5 collective-permute-start.2
  18.9 1.5 collective-permute-start.1
  20.4 2.7 %collective-permute-done.1.refs_2_ = s32[512]{0:T(512)S(1)} collective-permute-done((s32[512]{0:T(512)S(1)}, s32[512]{0:T(512)S(1)}, u32[]{:S(2)}, u32[]{:S(2)}) %collective-permute-start.1) | collective-permute-done | bytes 2080 | tf_op jit(solution)/shard_map/ppermute | solution.py:382
  23.1 1.4 all-to-all-done
  24.5 2.2 %copy-done = bf16[16384,128]{1,0:T(8,128)(2,1)S(1)} copy-done((bf16[16384,128]{1,0:T(8,128)(2,1)S(1)}, bf16[16384,128]{1,0:T(8,128)(2,1)}, u32[]{:S(2)}) %copy-start) | copy-done | bytes 4194328
  26.7 3.5 %pick_cold.1 = bf16[64,32,128]{2,1,0:T(8,128)(2,1)} custom-call(s32[64,32]{1,0:T(8,128)S(1)} %bitcast.23, bf16[16384,128]{1,0:T(8,128)(2,1)S(1)} %copy-done), custom_call_target="tpu_custom_call" | custom-call | bytes 4194304 | tf_op jit(solution)/shard_map/pick_cold/pallas_call | solution.py:314
  30.3 0.0 copy-start.9
  30.3 0.0 copy-start.10
  30.3 10.4 %all-to-all-start.1 = ((bf16[64,32,128]{2,1,0:T(8,128)(2,1)}), bf16[64,32,128]{2,1,0:T(8,128)(2,1)S(1)}, u32[]{:S(2)}, u32[]{:S(2)}) async-start(bf16[64,32,128]{2,1,0:T(8,128)(2,1)} %pick_cold.1), calls=%async_computation.1 | async-start | bytes 1048576 | tf_op jit(solution)/shard_map/all_to_all | solution.py:342
  40.7 0.0 copy-start.1
  40.7 2.2 %copy-done.1 = bf16[16384,128]{1,0:T(8,128)(2,1)S(1)} copy-done((bf16[16384,128]{1,0:T(8,128)(2,1)S(1)}, bf16[16384,128]{1,0:T(8,128)(2,1)}, u32[]{:S(2)}) %copy-start.1) | copy-done | bytes 4194328
  42.9 2.4 %pick_hot.1 = (bf16[512,128]{1,0:T(8,128)(2,1)S(1)}, bf16[512,128]{1,0:T(8,128)(2,1)S(1)}, bf16[512,128]{1,0:T(8,128)(2,1)S(1)}, bf16[512,128]{1,0:T(8,128)(2,1)S(1)}) custom-call(s32[512]{0:T(512)S(1)} %bitcast.25, s32[512]{0:T(512)S(1)} %collective-permute-done.refs_1_, s32[512]{0:T(512)S(1)} %collective-permute-done.1.refs_2_, ...), custom_call_target="tpu_custom_call" | custom-call | bytes 4194304 | tf_op jit(solution)/shard_map/pick_hot/pallas_call | solution.py:314
  45.3 1.3 collective-permute-start.3
  46.7 0.5 collective-permute-start.4
  47.2 0.6 collective-permute-start.5
  47.8 0.1 pad_add_fusion.where_hot
  47.9 8.4 %order.1.places = s32[11,1,8192]{2,1,0:T(1,128)S(1)} custom-call(s32[15,1,512]{2,1,0:T(1,128)S(1)} %bitcast.24, s32[10,1,7680]{2,1,0:T(1,128)S(1)} %bitcast.22, s32[1,7680]{1,0:T(1,128)S(1)} %copy-done.4), custom_call_target="tpu_custom_call" | custom-call | bytes 8388608 | tf_op jit(solution)/shard_map/order/pallas_call | solution.py:84
  56.3 0.1 collective-permute-done.5.hot3
  56.4 2.1 %all-to-all-done.1.cold = bf16[64,32,128]{2,1,0:T(8,128)(2,1)S(1)} async-done(((bf16[64,32,128]{2,1,0:T(8,128)(2,1)}), bf16[64,32,128]{2,1,0:T(8,128)(2,1)S(1)}, u32[]{:S(2)}, u32[]{:S(2)}) %all-to-all-start.1) | async-done | bytes 524320 | tf_op jit(solution)/shard_map/all_to_all | solution.py:342
  58.5 58.9 %train.1 = (f32[1,512]{1,0:T(1,128)}, f32[640,128]{1,0:T(8,128)S(1)}, f32[640,128]{1,0:T(8,128)S(1)}) custom-call(s32[64]{0:T(128)S(1)} %bitcast.28, s32[4]{0:T(128)S(1)} %pad_add_fusion.where_hot, s32[1]{0:T(128)} %bitcast.5.core, s32[11,1,8192]{2,1,0:T(1,128)S(1)} %order.1.places, bf16[512,128]{1,0:T(8,128)(2,1)S(1)} %get-tuple-element.44.hot0, ...), custom_call_target="tpu_custom_call" | custom-call | flops 4294967296 | bytes 4194304 | tf_op jit(solution)/shard_map/train/pallas_call | solution.py:255
  117.4 0.5 collective-permute-start.6
  117.9 1.3 collective-permute-done.6
  119.2 13.1 %all_to_all.32 = f32[16,5,8,128]{3,2,1,0:T(8,128)S(1)} all-to-all(f32[16,5,8,128]{3,2,1,0:T(8,128)S(1)} %bitcast.29), channel_id=1, replica_groups=mesh['clique'=4,'z'=8,'y'=4,'core'=2] {'clique','y'}, dimensions={0} | all-to-all | bytes 655360 | tf_op jit(solution)/shard_map/all_to_all | solution.py:342
  132.3 14.7 %all_to_all.33 = f32[8,5,8,128]{3,2,1,0:T(8,128)S(1)} all-to-all(f32[8,5,8,128]{3,2,1,0:T(8,128)S(1)} %broadcast_in_dim.7), channel_id=1, replica_groups=mesh['clique'=4,'z'=8,'y'=4,'core'=2] {'z'}, dimensions={0} | all-to-all | bytes 327680 | tf_op jit(solution)/shard_map/all_to_all | solution.py:342
  147.1 11.5 %all_to_all.34 = f32[16,5,8,128]{3,2,1,0:T(8,128)S(1)} all-to-all(f32[16,5,8,128]{3,2,1,0:T(8,128)S(1)} %broadcast_in_dim.8), channel_id=1, replica_groups=mesh['clique'=4,'z'=8,'y'=4,'core'=2] {'clique','y'}, dimensions={0} | all-to-all | bytes 655360 | tf_op jit(solution)/shard_map/all_to_all | solution.py:342
  158.5 4.3 %collective-permute-start.7 = (f32[640,128]{1,0:T(8,128)S(1)}, f32[640,128]{1,0:T(8,128)S(1)}, u32[]{:S(2)}, u32[]{:S(2)}) collective-permute-start(f32[640,128]{1,0:T(8,128)S(1)} %bitcast.20), channel_id=1, source_target_pairs={{0,1},{1,0},{2,3},{3,2},{4,5},{5,4},{6,7},{7,6},{8,9},{9,8},{10,11... | collective-permute-start | bytes 983048 | tf_op jit(solution)/shard_map/ppermute | solution.py:364
  162.9 1.3 collective-permute-done.7.other
  164.1 0.9 split.1
  (26 shorter events, 0.2 us)
Async XLA Ops:
  2.0 22.5 %all-to-all-start = ((s32[64,1,32]{2,1,0:T(1,128)}), s32[64,1,32]{2,1,0:T(1,128)S(1)}, u32[]{:S(2)}, u32[]{:S(2)}) async-start(s32[64,1,32]{2,1,0:T(1,128)} %bitcast.10), calls=%async_computation | async-start | bytes 65536 | tf_op jit(solution)/shard_map/all_to_all | solution.py:342
  16.1 4.3 %collective-permute-start = (s32[512]{0:T(512)S(1)}, s32[512]{0:T(512)S(1)}, u32[]{:S(2)}, u32[]{:S(2)}) collective-permute-start(s32[512]{0:T(512)S(1)} %bitcast.32), channel_id=1, source_target_pairs={{0,64},{64,128},{128,192},{192,0},{1,65},{65,129},{129,193},{193,1... | collective-permute-start | bytes 6152 | tf_op jit(solution)/shard_map/ppermute | solution.py:382
  17.4 3.0 %collective-permute-start.2 = (s32[512]{0:T(512)S(1)}, s32[512]{0:T(512)S(1)}, u32[]{:S(2)}, u32[]{:S(2)}) collective-permute-start(s32[512]{0:T(512)S(1)} %bitcast.31), channel_id=1, source_target_pairs={{0,192},{64,0},{128,64},{192,128},{1,193},{65,1},{129,65},{193,129... | collective-permute-start | bytes 6152 | tf_op jit(solution)/shard_map/ppermute | solution.py:382
  18.9 4.2 %collective-permute-start.1 = (s32[512]{0:T(512)S(1)}, s32[512]{0:T(512)S(1)}, u32[]{:S(2)}, u32[]{:S(2)}) collective-permute-start(s32[512]{0:T(512)S(1)} %bitcast.30), channel_id=1, source_target_pairs={{0,128},{64,192},{128,0},{192,64},{1,129},{65,193},{129,1},{193,65... | collective-permute-start | bytes 6152 | tf_op jit(solution)/shard_map/ppermute | solution.py:382
  24.5 2.2 %copy-start = (bf16[16384,128]{1,0:T(8,128)(2,1)S(1)}, bf16[16384,128]{1,0:T(8,128)(2,1)}, u32[]{:S(2)}) copy-start(bf16[16384,128]{1,0:T(8,128)(2,1)} %refs_1_.1) | copy-start | bytes 12582916
  26.7 21.2 %copy-start.2 = (s32[1,10,7680]{2,0,1:T(1,128)S(1)}, s32[1,10,7680]{2,0,1:T(1,128)}, u32[]{:S(2)}) copy-start(s32[1,10,7680]{2,0,1:T(1,128)} %param.19) | copy-start | bytes 921604
  26.7 21.2 %copy-start.3 = (s32[1,15,512]{2,0,1:T(1,128)S(1)}, s32[1,15,512]{2,0,1:T(1,128)}, u32[]{:S(2)}) copy-start(s32[1,15,512]{2,0,1:T(1,128)} %param.20) | copy-start | bytes 92164
  26.7 21.2 %copy-start.4 = (s32[1,7680]{1,0:T(1,128)S(1)}, s32[1,7680]{1,0:T(1,128)}, u32[]{:S(2)}) copy-start(s32[1,7680]{1,0:T(1,128)} %mid_self.1) | copy-start | bytes 92164
  30.3 28.2 %copy-start.5 = (bf16[256,172]{0,1:T(8,128)(2,1)S(1)}, bf16[256,172]{0,1:T(8,128)(2,1)}, u32[]{:S(2)}) copy-start(bf16[256,172]{0,1:T(8,128)(2,1)} %param.24) | copy-start | bytes 264196
  30.3 28.2 %copy-start.6 = (bf16[256,172]{0,1:T(8,128)(2,1)S(1)}, bf16[256,172]{0,1:T(8,128)(2,1)}, u32[]{:S(2)}) copy-start(bf16[256,172]{0,1:T(8,128)(2,1)} %param.25) | copy-start | bytes 264196
  30.3 28.2 %copy-start.7 = (bf16[128,256]{1,0:T(8,128)(2,1)S(1)}, bf16[128,256]{1,0:T(8,128)(2,1)}, u32[]{:S(2)}) copy-start(bf16[128,256]{1,0:T(8,128)(2,1)} %w1_self.1) | copy-start | bytes 196612
  30.3 28.2 %copy-start.8 = (bf16[128,256]{1,0:T(8,128)(2,1)S(1)}, bf16[128,256]{1,0:T(8,128)(2,1)}, u32[]{:S(2)}) copy-start(bf16[128,256]{1,0:T(8,128)(2,1)} %w1_neigh.1) | copy-start | bytes 196612
  30.3 28.2 %copy-start.9 = (s32[1,512]{1,0:T(1,128)S(1)}, s32[1,512]{1,0:T(1,128)}, u32[]{:S(2)}) copy-start(s32[1,512]{1,0:T(1,128)} %labels.1) | copy-start | bytes 6148
  30.3 28.2 %copy-start.10 = (s32[1,64]{1,0:T(1,128)S(1)}, s32[1,64]{1,0:T(1,128)}, u32[]{:S(2)}) copy-start(s32[1,64]{1,0:T(1,128)} %param.17) | copy-start | bytes 772
  30.3 28.2 %all-to-all-start.1 = ((bf16[64,32,128]{2,1,0:T(8,128)(2,1)}), bf16[64,32,128]{2,1,0:T(8,128)(2,1)S(1)}, u32[]{:S(2)}, u32[]{:S(2)}) async-start(bf16[64,32,128]{2,1,0:T(8,128)(2,1)} %pick_cold.1), calls=%async_computation.1 | async-start | bytes 1048576 | tf_op jit(solution)/shard_map/all_to_all | solution.py:342
  40.7 2.2 %copy-start.1 = (bf16[16384,128]{1,0:T(8,128)(2,1)S(1)}, bf16[16384,128]{1,0:T(8,128)(2,1)}, u32[]{:S(2)}) copy-start(bf16[16384,128]{1,0:T(8,128)(2,1)} %refs_4_.1) | copy-start | bytes 12582916
  45.3 11.0 %collective-permute-start.3 = (bf16[512,128]{1,0:T(8,128)(2,1)S(1)}, bf16[512,128]{1,0:T(8,128)(2,1)S(1)}, u32[]{:S(2)}, u32[]{:S(2)}) collective-permute-start(bf16[512,128]{1,0:T(8,128)(2,1)S(1)} %get-tuple-element.45), channel_id=1, source_target_pairs={{0,192},{64,0},{128,64},{192,128},{1,193},{65,1},{129,65},{193,129... | collective-permute-start | bytes 393224 | tf_op jit(solution)/shard_map/ppermute | solution.py:337
  46.7 9.6 %collective-permute-start.4 = (bf16[512,128]{1,0:T(8,128)(2,1)S(1)}, bf16[512,128]{1,0:T(8,128)(2,1)S(1)}, u32[]{:S(2)}, u32[]{:S(2)}) collective-permute-start(bf16[512,128]{1,0:T(8,128)(2,1)S(1)} %get-tuple-element.46), channel_id=1, source_target_pairs={{0,128},{64,192},{128,0},{192,64},{1,129},{65,193},{129,1},{193,65... | collective-permute-start | bytes 393224 | tf_op jit(solution)/shard_map/ppermute | solution.py:337
  47.2 9.2 %collective-permute-start.5 = (bf16[512,128]{1,0:T(8,128)(2,1)S(1)}, bf16[512,128]{1,0:T(8,128)(2,1)S(1)}, u32[]{:S(2)}, u32[]{:S(2)}) collective-permute-start(bf16[512,128]{1,0:T(8,128)(2,1)S(1)} %get-tuple-element.47), channel_id=1, source_target_pairs={{0,64},{64,128},{128,192},{192,0},{1,65},{65,129},{129,193},{193,1... | collective-permute-start | bytes 393224 | tf_op jit(solution)/shard_map/ppermute | solution.py:337
  117.4 1.8 %collective-permute-start.6 = (f32[640,128]{1,0:T(8,128)S(1)}, f32[640,128]{1,0:T(8,128)S(1)}, u32[]{:S(2)}, u32[]{:S(2)}) collective-permute-start(f32[640,128]{1,0:T(8,128)S(1)} %get-tuple-element.50), channel_id=1, source_target_pairs={{0,1},{1,0},{2,3},{3,2},{4,5},{5,4},{6,7},{7,6},{8,9},{9,8},{10,11... | collective-permute-start | bytes 983048 | tf_op jit(solution)/shard_map/ppermute | solution.py:360
  158.5 5.6 %collective-permute-start.7 = (f32[640,128]{1,0:T(8,128)S(1)}, f32[640,128]{1,0:T(8,128)S(1)}, u32[]{:S(2)}, u32[]{:S(2)}) collective-permute-start(f32[640,128]{1,0:T(8,128)S(1)} %bitcast.20), channel_id=1, source_target_pairs={{0,1},{1,0},{2,3},{3,2},{4,5},{5,4},{6,7},{7,6},{8,9},{9,8},{10,11... | collective-permute-start | bytes 983048 | tf_op jit(solution)/shard_map/ppermute | solution.py:364
